TPU v7x, 128 devices: a whole 4x4x4 slice. The times are simulated.
128 devices in a mesh: replica: 8 (over z, core), fsdp: 16 (over y, x).
Axes of the slice: x: 4, y: 4, z: 4, core: 2. Of those that a mesh axis runs over, the one named last changes fastest.
Arguments:
- grads: bfloat16 [8, 8192, 4096], P('replica', 'fsdp'), may hold values from -6 to 6
- owners: int32 [16, 8], P(None, 'replica'), may hold values from 0 to 31, as said below
- factors: bfloat16 [8, 16, 2, 2, 512, 512], P('replica', 'fsdp'), as said below
- momentum: bfloat16 [8, 16, 2, 512, 512], P('replica', 'fsdp'), may hold values from -6 to 6
- accum: float32 [8, 16, 2, 512, 512], P('replica', 'fsdp'), may hold values from 0.1 to 10
Outputs:
- update: bfloat16 [8192, 4096], P('fsdp')
- momentum_out: bfloat16 [8, 16, 2, 512, 512], P('replica', 'fsdp')
- accum_out: float32 [8, 16, 2, 512, 512], P('replica', 'fsdp')
Inputs may be any that keep to these rules, and one draw needn't show every extreme that they name: `owners`: each entry is f * 2 + s: slot s of fsdp index f within the replica index that holds the block's columns. Within one replica index no slot is named twice, some fsdp index has all 2 of its slots named, and both the first and the last slot are named. Each of the two factors of a slot is symmetric and positive definite.
All inputs are finite; a program needn't handle non-finite values.
Results may differ from a plain program's by a relative error of at most 0.029.
Values may be sent and summed in bfloat16 or wider, within the bound.
No kernel may reach another device: no remote copies, remote signals or barrier semaphores. Data moves between devices by JAX's collectives and lax.ppermute only.
A program may use at most 128 MiB of HBM per device.

v0:
```python
import jax
import jax.numpy as jnp
from jax import lax
from jax.sharding import PartitionSpec as P


def slot_step(grad_block, left, right, moment, squares):
    squares_new = squares + grad_block * grad_block
    adagrad = grad_block / jnp.sqrt(squares_new)
    inner = jnp.dot(left.astype(jnp.float32), grad_block, precision=lax.Precision.HIGHEST)
    precond = jnp.dot(inner, right.astype(jnp.float32), precision=lax.Precision.HIGHEST)
    ratio = jnp.sqrt(jnp.sum(adagrad * adagrad)) / jnp.sqrt(jnp.sum(precond * precond) + 1e-06)
    step = precond * ratio
    moment_new = (0.9 * moment.astype(jnp.float32) + step).astype(jnp.bfloat16)
    kept = lax.optimization_barrier(moment_new)
    update = (0.9 * kept.astype(jnp.float32) + step).astype(jnp.bfloat16)
    return (moment_new, squares_new, update)


def body(grads, owners, factors, momentum, accum):
    side = factors.shape[-1]
    slot_count = factors.shape[2]
    row_span = grads.shape[1]
    group_cols = owners.shape[1]
    col_span = group_cols * side
    row_blocks = row_span // side
    home_count = row_blocks * group_cols
    peers = lax.axis_size("fsdp")
    position = lax.axis_index("fsdp")
    summed = lax.psum(grads[0].astype(jnp.float32).astype(jnp.bfloat16), "replica").astype(
        jnp.float32
    )
    mine = lax.dynamic_slice_in_dim(summed, lax.axis_index("replica") * col_span, col_span, 1)
    home_blocks = mine.astype(jnp.bfloat16).reshape(row_blocks, side, group_cols, side)
    home_blocks = home_blocks.transpose(0, 2, 1, 3).reshape(home_count, side, side)
    slot_ids = owners.reshape(-1)
    targets = position * slot_count + jnp.arange(slot_count, dtype=jnp.int32)
    my_ids = lax.dynamic_slice_in_dim(slot_ids, position * home_count, home_count)
    owner_fsdp = my_ids // slot_count
    routing = jnp.arange(peers, dtype=jnp.int32)[:, None] == owner_fsdp[None, :]
    outgoing = jnp.where(routing[:, :, None, None], home_blocks[None], jnp.zeros((), jnp.bfloat16))
    incoming = lax.all_to_all(outgoing, "fsdp", split_axis=0, concat_axis=0, tiled=True)
    picker = (slot_ids[None, :] == targets[:, None]).astype(jnp.bfloat16)
    slot_grad = jnp.dot(
        picker,
        incoming.reshape(peers * home_count, side * side),
        preferred_element_type=jnp.float32,
    )
    slot_grad = slot_grad.reshape(slot_count, side, side)
    moment_new, squares_new, slot_update = jax.vmap(slot_step)(
        slot_grad, factors[0, 0, :, 0], factors[0, 0, :, 1], momentum[0, 0], accum[0, 0]
    )
    update_flat = slot_update.reshape(slot_count, side * side)
    placer = (slot_ids[:, None] == targets[None, :]).astype(jnp.bfloat16)
    outgoing_back = jnp.dot(placer, update_flat, preferred_element_type=jnp.float32).astype(
        jnp.bfloat16
    )
    arrived = lax.all_to_all(
        outgoing_back.reshape(peers, home_count, side, side),
        "fsdp",
        split_axis=0,
        concat_axis=0,
        tiled=True,
    )
    home_update = jnp.take_along_axis(arrived, owner_fsdp[None, :, None, None], 0)[0]
    tile = (
        home_update.reshape(row_blocks, group_cols, side, side)
        .transpose(0, 2, 1, 3)
        .reshape(row_span, col_span)
    )
    update = lax.all_gather(tile, "replica", axis=1, tiled=True)
    return (update, moment_new[None, None], squares_new[None, None])


def solution(mesh):
    in_specs = (
        P("replica", "fsdp", None),
        P(None, "replica"),
        P("replica", "fsdp", None, None, None, None),
        P("replica", "fsdp", None, None, None),
        P("replica", "fsdp", None, None, None),
    )
    out_specs = (
        P("fsdp", None),
        P("replica", "fsdp", None, None, None),
        P("replica", "fsdp", None, None, None),
    )
    return jax.shard_map(body, mesh=mesh, in_specs=in_specs, out_specs=out_specs, check_vma=False)
```

profile of v0, /device:TPU:1, one launch (start us, length us, event | category | flops | bytes accessed | tf_op | source)
XLA Modules:
  0.0 434.9 jit_solution(11373140291307367755)
XLA Ops:
  7.2 0.0 all-reduce.2.cloned.1.call-start
  7.2 0.0 copy-start.4
  7.2 0.7 all-reduce.2.cloned.1.call-update
  7.9 0.0 copy-done.4
  7.9 0.6 constant_dynamic-slice_fusion
  11.1 73.7 %all-reduce.2.cloned.1.call-done = bf16[512,4096]{1,0:T(8,128)(2,1)} async-done(((bf16[512,4096]{1,0:T(8,128)(2,1)}), bf16[512,4096]{1,0:T(8,128)(2,1)}) %all-reduce.2.cloned.1.call-update) | async-done | bytes 4194320 | tf_op jit(solution)/shard_map/psum | solution.py:30
  84.8 1.1 convert_convert_fusion
  85.9 4.0 broadcast_select_fusion
  89.9 6.6 %all-to-all-start = ((bf16[16,1,512,512]{3,2,1,0:T(8,128)(2,1)}), bf16[16,1,512,512]{3,2,1,0:T(8,128)(2,1)}, u32[]{:S(2)}, u32[]{:S(2)}) async-start(bf16[16,1,512,512]{3,2,1,0:T(8,128)(2,1)} %broadcast_select_fusion), calls=%async_computation | async-start | bytes 16777216 | tf_op jit(solution)/shard_map/all_to_all | solution.py:42
  96.5 119.8 %all-to-all-done = bf16[16,1,512,512]{3,2,1,0:T(8,128)(2,1)} async-done(((bf16[16,1,512,512]{3,2,1,0:T(8,128)(2,1)}), bf16[16,1,512,512]{3,2,1,0:T(8,128)(2,1)}, u32[]{:S(2)}, u32[]{:S(2)}) %all-to-all-start) | async-done | bytes 8388640 | tf_op jit(solution)/shard_map/all_to_all | solution.py:42
  216.2 0.0 copy-start.2
  216.3 8.6 %fusion = f32[2,512,512]{2,0,1:T(2,128)S(1)} fusion(s32[16]{0:T(128)S(1)} %bitcast.65, s32[2]{0:T(128)S(1)} %iota_add_fusion, bf16[2,8,512,512]{3,2,1,0:T(8,128)(2,1)} %bitcast.24), kind=kOutput, calls=%fused_computation.1 | convolution fusion | flops 16777248 | bytes 10485832 | tf_op jit(solution)/shard_map/dot_general | solution.py:44
  224.8 0.0 copy-done.2
  224.8 2.0 fusion.4
  226.9 0.0 copy-start.1
  226.9 2.1 multiply_reduce_fusion
  228.9 0.0 copy-done.1
  228.9 0.0 copy-start.3
  228.9 5.3 %fusion.12 = (f32[1,1,2,512,512]{4,2,3,1,0:T(2,128)S(1)}, f32[2]{0:T(128)S(1)}) fusion(f32[2,512,512]{2,0,1:T(2,128)S(1)} %fusion, f32[1,1,2,512,512]{4,3,2,1,0:T(8,128)S(1)} %copy-done.1), kind=kLoop, calls=%fused_computation.20 | loop fusion | flops 2621438 | bytes 6291464 | tf_op jit(solution)/shard_map/broadcast_in_dim | solution.py:72
  234.3 0.0 copy-done.3
  234.3 0.4 fusion.3
  234.7 0.0 copy-start
  234.8 0.4 fusion.6
  235.2 0.5 copy-done
  235.7 1.1 copy.30
  236.8 5.6 %convolution_convert_fusion = bf16[16,262144]{1,0:T(8,128)(2,1)} fusion(bf16[2,262144]{1,0:T(2,128)(2,1)S(1)} %bitcast.62, s32[2]{0:T(128)S(1)} %iota_add_fusion, s32[16]{0:T(128)S(1)} %bitcast.66), kind=kOutput, calls=%fused_computation | convolution fusion | flops 20971552 | bytes 9437256 | tf_op jit(solution)/shard_map/dot_general | solution.py:55
  242.4 9.6 %copy.31 = bf16[2,8,512,512]{3,2,1,0:T(8,128)(2,1)} copy(bf16[2,8,512,512]{3,1,2,0:T(8,128)(2,1)} %bitcast.60) | data formatting | bytes 16777216
  252.0 4.8 %all-to-all-start.1 = ((bf16[16,1,512,512]{3,2,1,0:T(8,128)(2,1)}), bf16[16,1,512,512]{3,2,1,0:T(8,128)(2,1)}, u32[]{:S(2)}, u32[]{:S(2)}) async-start(bf16[16,1,512,512]{3,2,1,0:T(8,128)(2,1)} %bitcast.59), calls=%async_computation.1 | async-start | bytes 16777216 | tf_op jit(solution)/shard_map/all_to_all | solution.py:58
  256.8 0.0 all-gather.3.cloned.1.call-start
  256.9 117.1 %all-to-all-done.1 = bf16[16,1,512,512]{3,2,1,0:T(8,128)(2,1)} async-done(((bf16[16,1,512,512]{3,2,1,0:T(8,128)(2,1)}), bf16[16,1,512,512]{3,2,1,0:T(8,128)(2,1)}, u32[]{:S(2)}, u32[]{:S(2)}) %all-to-all-start.1) | async-done | bytes 8388640 | tf_op jit(solution)/shard_map/all_to_all | solution.py:58
  374.0 1.9 dynamic-slice_select_fusion
  375.9 0.0 all-gather.3.cloned.1.call-update
  375.9 1.7 copy.24
  377.6 45.7 %all-gather.3.cloned.1.call-done = bf16[1,1,512,4096]{3,2,1,0:T(8,128)(2,1)} async-done(((bf16[1,1,512,512]{3,2,1,0:T(8,128)(2,1)}), bf16[1,1,512,4096]{3,2,1,0:T(8,128)(2,1)}) %all-gather.3.cloned.1.call-update) | async-done | bytes 4194320 | tf_op jit(solution)/shard_map/all_gather | solution.py:71
  423.4 4.7 %copy.49 = bf16[512,4096]{1,0:T(8,128)(2,1)} copy(bf16[512,4096]{1,0:T(8,128)(2,1)} %bitcast.64) | data formatting | bytes 8388608
  (3 shorter events, 0.0 us)
Async XLA Ops:
  7.2 77.7 %all-reduce.2.cloned.1.call-start = ((), (), s32[]{:S(2)}) async-start(), calls=%async_computation.2 | async-start | bytes 8388608 | tf_op jit(solution)/shard_map/psum | solution.py:30
  7.2 0.7 copy-start.4
  89.9 126.4 %all-to-all-start = ((bf16[16,1,512,512]{3,2,1,0:T(8,128)(2,1)}), bf16[16,1,512,512]{3,2,1,0:T(8,128)(2,1)}, u32[]{:S(2)}, u32[]{:S(2)}) async-start(bf16[16,1,512,512]{3,2,1,0:T(8,128)(2,1)} %broadcast_select_fusion), calls=%async_computation | async-start | bytes 16777216 | tf_op jit(solution)/shard_map/all_to_all | solution.py:42
  216.2 8.6 %copy-start.2 = (bf16[1,1,2,2,512,512]{5,4,3,2,1,0:T(8,128)(2,1)S(1)}, bf16[1,1,2,2,512,512]{5,4,3,2,1,0:T(8,128)(2,1)}, u32[]{:S(2)}) copy-start(bf16[1,1,2,2,512,512]{5,4,3,2,1,0:T(8,128)(2,1)} %param.7) | copy-start | bytes 6291460
  226.9 2.1 copy-start.1
  228.9 5.4 %copy-start.3 = (bf16[1,1,2,512,512]{4,3,2,1,0:T(8,128)(2,1)S(1)}, bf16[1,1,2,512,512]{4,3,2,1,0:T(8,128)(2,1)}, u32[]{:S(2)}) copy-start(bf16[1,1,2,512,512]{4,3,2,1,0:T(8,128)(2,1)} %param.8) | copy-start | bytes 3145732
  234.7 1.0 copy-start
  252.0 122.0 %all-to-all-start.1 = ((bf16[16,1,512,512]{3,2,1,0:T(8,128)(2,1)}), bf16[16,1,512,512]{3,2,1,0:T(8,128)(2,1)}, u32[]{:S(2)}, u32[]{:S(2)}) async-start(bf16[16,1,512,512]{3,2,1,0:T(8,128)(2,1)} %bitcast.59), calls=%async_computation.1 | async-start | bytes 16777216 | tf_op jit(solution)/shard_map/all_to_all | solution.py:58
  256.8 166.6 %all-gather.3.cloned.1.call-start = ((), (), s32[]{:S(2)}) async-start(), calls=%async_computation.3 | async-start | bytes 4718592 | tf_op jit(solution)/shard_map/all_gather | solution.py:71
Sparse Core Ops, SparseCore 0:
  10.4 74.4 all-reduce.1
  376.1 47.2 all-gather.2
where the time goes:
time: 435 us
  waiting for transfers between devices  357 us (82%)
  matrix products  18.3 us (4%)
  local copies, waits for them, and re-layouts  18.2 us (4%)
  between operations  16.8 us (4%)
  other arithmetic  13.2 us (3%)
  starting transfers between devices  11.4 us (3%)
    all_to_all x1, waiting for transfers between devices, body(): lax.all_to_all(outgoing, 'fsdp', split_axis=0, concat_axis=0, tiled=True)  120 us
    all_to_all x1, waiting for transfers between devices, body(): lax.all_to_all(outgoing_back.reshape(peers, home_count, side, side), 'fsd...  117 us
    psum x1, waiting for transfers between devices, body(): lax.psum(grads[0].astype(jnp.float32).astype(jnp.bfloat16), 'replica')  73.7 us
    all_gather x1, waiting for transfers between devices, body(): update = lax.all_gather(tile, 'replica', axis=1, tiled=True)  45.7 us
    unnamed x14, local copies, waits for them, and re-layouts  17.6 us
  transfers between devices with their start and end apart: 4, of which 4 were waited for; matrix products, arithmetic and copies ran while one was open for 1% of the time, Pallas kernels for 0%

commit v1 on v0

v1 whole, which is shorter than its diff:
```python
import jax
import jax.numpy as jnp
from jax import lax
from jax.experimental import pallas as pl
from jax.experimental.pallas import tpu as pltpu
from jax.sharding import PartitionSpec as P

SIDE = 512
SLOTS = 2
PEERS = 16
PIECE = SIDE // PEERS
HALF = SIDE // 2
VMEM_LIMIT = 48 * 1024 * 1024


def ring(step):
    return [(i, ((i // 2 + step) % 4) * 2 + i % 2) for i in range(8)]


UP = ring(1)
DOWN = ring(3)
CORES = [(i, i ^ 1) for i in range(8)]


def add(a, b):
    return (a.astype(jnp.float32) + b.astype(jnp.float32)).astype(jnp.bfloat16)


def sum_replicas(grads, z, core):
    def part(d, which):
        col = (lax.rem(z + d, 4) * 2 + which) * SIDE
        return lax.dynamic_slice(grads, (0, col), (SIDE, SIDE))

    give = jnp.stack([part(d, 1 - core) for d in (2, 1, 3, 0)])
    got = lax.ppermute(give, "replica", CORES)
    s = {d: add(part(d, core), got[n]) for n, d in enumerate((2, 1, 3, 0))}
    up1 = lax.ppermute(s[2][:HALF], "replica", UP)
    down1 = lax.ppermute(s[2][HALF:], "replica", DOWN)
    up2 = lax.ppermute(s[1][HALF:], "replica", UP)
    down2 = lax.ppermute(s[3][:HALF], "replica", DOWN)
    up3 = lax.ppermute(add(s[1][:HALF], up1), "replica", UP)
    down3 = lax.ppermute(add(s[3][HALF:], down1), "replica", DOWN)
    own = s[0].astype(jnp.float32)
    top = own[:HALF] + down2.astype(jnp.float32) + up3.astype(jnp.float32)
    low = own[HALF:] + up2.astype(jnp.float32) + down3.astype(jnp.float32)
    return jnp.concatenate([top, low]).astype(jnp.bfloat16)


def pick_kernel(index_ref, x_ref, o_ref):
    for t in range(o_ref.shape[0]):
        i = index_ref[t]
        v = x_ref[jnp.maximum(i, 0)]
        o_ref[t] = jnp.where(i >= 0, v, jnp.zeros_like(v))


def pick(index, x, count):
    return pl.pallas_call(
        pick_kernel,
        out_shape=jax.ShapeDtypeStruct((count,) + x.shape[1:], x.dtype),
        in_specs=[
            pl.BlockSpec(memory_space=pltpu.SMEM),
            pl.BlockSpec(memory_space=pltpu.VMEM),
        ],
        out_specs=pl.BlockSpec(memory_space=pltpu.VMEM),
        compiler_params=pltpu.CompilerParams(vmem_limit_bytes=VMEM_LIMIT),
        name="pick",
    )(index, x)


def slot_kernel(g_ref, f_ref, m_ref, a_ref, mo_ref, ao_ref, u_ref):
    g = g_ref[...].reshape(SIDE, SIDE)
    gf = g.astype(jnp.float32)
    squares = gf * gf
    accum = a_ref[0] + squares
    ao_ref[0] = accum
    adagrad = jnp.sum(squares / accum)
    inner = jnp.dot(f_ref[0, 0], g, preferred_element_type=jnp.float32)
    precond = jnp.dot(
        inner.astype(jnp.bfloat16), f_ref[0, 1], preferred_element_type=jnp.float32
    )
    norm = jnp.sum(precond * precond) + 1e-06
    step = precond * (jnp.sqrt(adagrad) / jnp.sqrt(norm))
    moment = (0.9 * m_ref[0].astype(jnp.float32) + step).astype(jnp.bfloat16)
    mo_ref[0] = moment
    update = (0.9 * moment.astype(jnp.float32) + step).astype(jnp.bfloat16)
    u_ref[...] = update.reshape(u_ref.shape)


def slot_step(g, factors, momentum, accum):
    block = (1, SIDE, SIDE)
    pieces = pl.BlockSpec((PEERS, 1, PIECE, SIDE), lambda s: (0, s, 0, 0))
    flat = pl.BlockSpec(block, lambda s: (s, 0, 0))
    return pl.pallas_call(
        slot_kernel,
        grid=(SLOTS,),
        out_shape=(
            jax.ShapeDtypeStruct(momentum.shape, momentum.dtype),
            jax.ShapeDtypeStruct(accum.shape, accum.dtype),
            jax.ShapeDtypeStruct(g.shape, jnp.bfloat16),
        ),
        in_specs=[
            pieces,
            pl.BlockSpec((1, 2, SIDE, SIDE), lambda s: (s, 0, 0, 0)),
            flat,
            flat,
        ],
        out_specs=(flat, flat, pieces),
        compiler_params=pltpu.CompilerParams(vmem_limit_bytes=VMEM_LIMIT),
        name="slot_step",
    )(g, factors, momentum, accum)


def gather_replicas(tile, z, core):
    top, low = tile[:HALF], tile[HALF:]
    own = lax.ppermute(tile, "replica", CORES)
    up1 = lax.ppermute(top, "replica", UP)
    down1 = lax.ppermute(low, "replica", DOWN)
    up2 = lax.ppermute(low, "replica", UP)
    down2 = lax.ppermute(top, "replica", DOWN)
    up3 = lax.ppermute(up1, "replica", UP)
    down3 = lax.ppermute(down1, "replica", DOWN)
    out = jnp.zeros((SIDE, 8 * SIDE), tile.dtype)
    for d, pair in ((3, (up1, up2)), (1, (down2, down1)), (2, (up3, down3))):
        col = lax.rem(z + d, 4) * 2 * SIDE
        for n, half in enumerate(pair):
            other = lax.ppermute(half, "replica", CORES)
            out = lax.dynamic_update_slice(out, half, (n * HALF, col + core * SIDE))
            out = lax.dynamic_update_slice(out, other, (n * HALF, col + (1 - core) * SIDE))
    out = lax.dynamic_update_slice(out, tile, (0, z * 2 * SIDE + core * SIDE))
    return lax.dynamic_update_slice(out, own, (0, z * 2 * SIDE + (1 - core) * SIDE))


def body(grads, owners, factors, momentum, accum):
    replica = lax.axis_index("replica")
    z, core = replica // 2, lax.rem(replica, 2)
    ids = owners[:, 0]
    named = ids[None, :] == jnp.arange(PEERS * SLOTS, dtype=jnp.int32)[:, None]
    block_of = jnp.max(
        jnp.where(named, jnp.arange(PEERS, dtype=jnp.int32)[None, :], -1), axis=1
    )

    home = sum_replicas(grads[0], z, core)
    pieces = lax.all_to_all(home.reshape(PEERS, PIECE, SIDE), "fsdp", 0, 0, tiled=True)
    routed = pick(block_of, pieces, PEERS * SLOTS)
    slot_grad = lax.all_to_all(
        routed.reshape(PEERS, SLOTS, PIECE, SIDE), "fsdp", 0, 0, tiled=True
    )
    moment_new, squares_new, update = slot_step(
        slot_grad, factors[0, 0], momentum[0, 0], accum[0, 0]
    )
    back = lax.all_to_all(update, "fsdp", 0, 0, tiled=True)
    back = pick(ids, back.reshape(PEERS * SLOTS, PIECE, SIDE), PEERS)
    tile = lax.all_to_all(back, "fsdp", 0, 0, tiled=True).reshape(SIDE, SIDE)
    out = gather_replicas(tile, z, core)
    return (out, moment_new[None, None], squares_new[None, None])


def solution(mesh):
    in_specs = (
        P("replica", "fsdp", None),
        P(None, "replica"),
        P("replica", "fsdp", None, None, None, None),
        P("replica", "fsdp", None, None, None),
        P("replica", "fsdp", None, None, None),
    )
    out_specs = (
        P("fsdp", None),
        P("replica", "fsdp", None, None, None),
        P("replica", "fsdp", None, None, None),
    )
    return jax.shard_map(body, mesh=mesh, in_specs=in_specs, out_specs=out_specs, check_vma=False)
```

time: 435 us -> 135 us (0.31)
  waiting for transfers between devices: 357 us -> 34.5 us
  blocking collectives: 0 us -> 45.4 us
  starting transfers between devices: 11.4 us -> 37.8 us
  matrix products: 18.3 us -> 0 us
  between operations: 16.8 us -> 1 us
  local copies, waits for them, and re-layouts: 18.2 us -> 4.75 us
  other arithmetic: 13.2 us -> 5.02 us
  Pallas kernels: 0 us -> 6.5 us
    all_to_all x2 -> x1, waiting for transfers between devices: 237 us -> 9.89 us  [body(): lax.all_to_all(home.reshape(PEERS, PIECE, SIDE), 'fsdp', 0, 0, tiled=True)]
    psum x1 -> x0, waiting for transfers between devices: 73.7 us -> none  [body(): lax.psum(grads[0].astype(jnp.float32).astype(jnp.bfloat16), 'replica')]
    all_gather x1 -> x0, waiting for transfers between devices: 45.7 us -> none  [body(): update = lax.all_gather(tile, 'replica', axis=1, tiled=True)]
    all_to_all x0 -> x3, blocking collectives: none -> 45.4 us  [the longest x1 17.4 us: body(): lax.all_to_all(routed.reshape(PEERS, SLOTS, PIECE, SIDE), 'fsdp', 0, 0, t...]
    ppermute x0 -> x20, starting transfers between devices: none -> 31 us  [the longest x6 12.5 us: gather_replicas(): other = lax.ppermute(half, 'replica', CORES)]
    ppermute x0 -> x20, waiting for transfers between devices: none -> 24.6 us  [the longest x1 4 us: sum_replicas(): got = lax.ppermute(give, 'replica', CORES)]
    dot_general x4 -> x0, matrix products: 18.3 us -> none  [the longest x1 8.58 us: body(): jnp.dot(picker, incoming.reshape(peers * home_count, side * side), prefer...]
    unnamed x14 -> x8, local copies, waits for them, and re-layouts: 17.6 us -> 2.03 us
  transfers between devices with their start and end apart: 4 -> 21, of which waited for: 4 -> 11; matrix products, arithmetic and copies ran while one was open for 1% -> 1% of each run, Pallas kernels for 0% -> 0%
where the time goes in v1:
time: 135 us
  blocking collectives  45.4 us (34%)
  starting transfers between devices  37.8 us (28%)
  waiting for transfers between devices  34.5 us (26%)
  Pallas kernels  6.5 us (5%)
  other arithmetic  5.02 us (4%)
  local copies, waits for them, and re-layouts  4.75 us (4%)
    all_to_all x1, blocking collectives, body(): lax.all_to_all(routed.reshape(PEERS, SLOTS, PIECE, SIDE), 'fsdp', 0, 0, t...  17.4 us
    all_to_all x1, blocking collectives, body(): back = lax.all_to_all(update, 'fsdp', 0, 0, tiled=True)  16 us
    ppermute x6, starting transfers between devices, gather_replicas(): other = lax.ppermute(half, 'replica', CORES)  12.5 us
    all_to_all x1, blocking collectives, body(): tile = lax.all_to_all(back, 'fsdp', 0, 0, tiled=True).reshape(SIDE, SIDE)  12 us
    all_to_all x1, waiting for transfers between devices, body(): lax.all_to_all(home.reshape(PEERS, PIECE, SIDE), 'fsdp', 0, 0, tiled=True)  9.89 us
    all_to_all x1, starting transfers between devices, body(): lax.all_to_all(home.reshape(PEERS, PIECE, SIDE), 'fsdp', 0, 0, tiled=True)  6.75 us
    pallas_call x1, Pallas kernels, slot_step(): pl.pallas_call(slot_kernel, grid=(SLOTS,), out_shape=(jax.ShapeDtypeStruc...  5.21 us
    ppermute x1, waiting for transfers between devices, sum_replicas(): got = lax.ppermute(give, 'replica', CORES)  4 us
  transfers between devices with their start and end apart: 21, of which 11 were waited for; matrix products, arithmetic and copies ran while one was open for 1% of the time, Pallas kernels for 0%

profile of v1, /device:TPU:1, one launch (start us, length us, event | category | flops | bytes accessed | tf_op | source)
XLA Modules:
  0.0 135.0 jit_solution(8713325178280087987)
XLA Ops:
  0.7 1.7 %constant_dynamic-slice_fusion.3 = (bf16[1,512,512]{2,1,0:T(8,128)(2,1)S(1)}, bf16[1,512,512]{2,1,0:T(8,128)(2,1)S(1)}, bf16[1,512,512]{2,1,0:T(8,128)(2,1)S(1)}, bf16[1,512,512]{2,1,0:T(8,128)(2,1)S(1)}) fusion(bf16[1,512,4096]{2,1,0:T(8,128)(2,1)} %param.5, s32[]{:T(128)S(6)} %select_n.66, s32[]{:T(128)S(6)} %select_n.69, s32[]{:T(128)S(6)} %select_n.68, ...), kind=kLoop, calls=%fused_computation.38 | loop fusion | bytes 4194320 | tf_op jit(solution)/shard_map/dynamic_slice | solution.py:32
  2.4 1.6 %pad_maximum_fusion = bf16[4,512,512]{2,1,0:T(8,128)(2,1)} fusion(bf16[1,512,512]{2,1,0:T(8,128)(2,1)S(1)} %get-tuple-element.14, bf16[1,512,512]{2,1,0:T(8,128)(2,1)S(1)} %get-tuple-element.15, bf16[1,512,512]{2,1,0:T(8,128)(2,1)S(1)} %get-tuple-element.16, bf16[1,512,512]{2,1,0:T(8,128)(2,1)S(1)} %get-tuple-element.13), kind=kLoop, calls=%fused_computation | loop fusion | flops 3145728 | bytes 4194304 | tf_op jit(solution)/shard_map/stack | solution.py:34
  4.0 1.4 %collective-permute-start = (bf16[4,512,512]{2,1,0:T(8,128)(2,1)}, bf16[4,512,512]{2,1,0:T(8,128)(2,1)S(1)}, u32[]{:S(2)}, u32[]{:S(2)}) collective-permute-start(bf16[4,512,512]{2,1,0:T(8,128)(2,1)} %pad_maximum_fusion), channel_id=1, source_target_pairs={{0,16},{16,0},{32,48},{48,32},{64,80},{80,64},{96,112},{112,96},{1... | collective-permute-start | bytes 6291464 | tf_op jit(solution)/shard_map/ppermute | solution.py:35
  5.4 4.0 %collective-permute-done = bf16[4,512,512]{2,1,0:T(8,128)(2,1)S(1)} collective-permute-done((bf16[4,512,512]{2,1,0:T(8,128)(2,1)}, bf16[4,512,512]{2,1,0:T(8,128)(2,1)S(1)}, u32[]{:S(2)}, u32[]{:S(2)}) %collective-permute-start) | collective-permute-done | bytes 2097184 | tf_op jit(solution)/shard_map/ppermute | solution.py:35
  9.4 2.1 %add_convert_fusion.1 = (bf16[1,512,512]{2,1,0:T(8,128)(2,1)S(1)}, bf16[1,512,512]{2,1,0:T(8,128)(2,1)S(1)}, bf16[1,512,512]{2,1,0:T(8,128)(2,1)S(1)}, f32[1,512,512]{2,1,0:T(8,128)S(1)}) fusion(bf16[4,512,512]{2,1,0:T(8,128)(2,1)S(1)} %collective-permute-done, bf16[1,512,4096]{2,1,0:T(8,128)(2,1)} %param.5, s32[]{:T(128)S(6)} %select_n.71, s32[]{:T(128)S(6)} %select_n.72, ...), kind=kLoop, calls=%fused_computation.2 | loop fusion | flops 4456448 | bytes 6815760 | tf_op jit(solution)/shard_map/convert_element_type | solution.py:26
  11.6 3.9 %collective-permute-start.5 = (bf16[256,512]{1,0:T(8,128)(2,1)S(1)}, bf16[256,512]{1,0:T(8,128)(2,1)S(1)}, u32[]{:S(2)}, u32[]{:S(2)}) collective-permute-start(bf16[256,512]{1,0:T(8,128)(2,1)S(1)} %get-tuple-element.22), channel_id=1, source_target_pairs={{0,96},{16,112},{32,0},{48,16},{64,32},{80,48},{96,64},{112,80},{1... | collective-permute-start | bytes 786440 | tf_op jit(solution)/shard_map/ppermute | solution.py:38
  15.5 2.7 %collective-permute-start.1 = (bf16[256,512]{1,0:T(8,128)(2,1)S(1)}, bf16[256,512]{1,0:T(8,128)(2,1)S(1)}, u32[]{:S(2)}, u32[]{:S(2)}) collective-permute-start(bf16[256,512]{1,0:T(8,128)(2,1)S(1)} %slice_bitcast_fusion.7), channel_id=1, source_target_pairs={{0,96},{16,112},{32,0},{48,16},{64,32},{80,48},{96,64},{112,80},{1... | collective-permute-start | bytes 786440 | tf_op jit(solution)/shard_map/ppermute | solution.py:40
  18.3 0.1 collective-permute-start.4
  18.4 2.5 %collective-permute-done.5 = bf16[256,512]{1,0:T(8,128)(2,1)S(1)} collective-permute-done((bf16[256,512]{1,0:T(8,128)(2,1)S(1)}, bf16[256,512]{1,0:T(8,128)(2,1)S(1)}, u32[]{:S(2)}, u32[]{:S(2)}) %collective-permute-start.5) | collective-permute-done | bytes 262176 | tf_op jit(solution)/shard_map/ppermute | solution.py:38
  20.8 0.1 fusion.7
  20.9 3.5 %collective-permute-start.6 = (bf16[256,512]{1,0:T(8,128)(2,1)S(1)}, bf16[256,512]{1,0:T(8,128)(2,1)S(1)}, u32[]{:S(2)}, u32[]{:S(2)}) collective-permute-start(bf16[256,512]{1,0:T(8,128)(2,1)S(1)} %fusion.7), channel_id=1, source_target_pairs={{0,96},{16,112},{32,0},{48,16},{64,32},{80,48},{96,64},{112,80},{1... | collective-permute-start | bytes 786440 | tf_op jit(solution)/shard_map/ppermute | solution.py:42
  24.4 0.1 fusion.8
  24.4 0.1 collective-permute-start.3
  24.5 1.9 %collective-permute-done.1 = bf16[256,512]{1,0:T(8,128)(2,1)S(1)} collective-permute-done((bf16[256,512]{1,0:T(8,128)(2,1)S(1)}, bf16[256,512]{1,0:T(8,128)(2,1)S(1)}, u32[]{:S(2)}, u32[]{:S(2)}) %collective-permute-start.1) | collective-permute-done | bytes 262176 | tf_op jit(solution)/shard_map/ppermute | solution.py:40
  26.4 3.1 %collective-permute-done.4 = bf16[256,512]{1,0:T(8,128)(2,1)S(1)} collective-permute-done((bf16[256,512]{1,0:T(8,128)(2,1)S(1)}, bf16[256,512]{1,0:T(8,128)(2,1)S(1)}, u32[]{:S(2)}, u32[]{:S(2)}) %collective-permute-start.4) | collective-permute-done | bytes 262176 | tf_op jit(solution)/shard_map/ppermute | solution.py:39
  29.5 2.5 %collective-permute-done.6 = bf16[256,512]{1,0:T(8,128)(2,1)S(1)} collective-permute-done((bf16[256,512]{1,0:T(8,128)(2,1)S(1)}, bf16[256,512]{1,0:T(8,128)(2,1)S(1)}, u32[]{:S(2)}, u32[]{:S(2)}) %collective-permute-start.6) | collective-permute-done | bytes 262176 | tf_op jit(solution)/shard_map/ppermute | solution.py:42
  32.0 3.1 %collective-permute-done.3 = bf16[256,512]{1,0:T(8,128)(2,1)S(1)} collective-permute-done((bf16[256,512]{1,0:T(8,128)(2,1)S(1)}, bf16[256,512]{1,0:T(8,128)(2,1)S(1)}, u32[]{:S(2)}, u32[]{:S(2)}) %collective-permute-start.3) | collective-permute-done | bytes 262176 | tf_op jit(solution)/shard_map/ppermute | solution.py:41
  35.1 0.3 fusion.6
  35.4 0.8 pad_maximum_fusion.1
  36.2 6.8 %all-to-all-start = ((bf16[16,32,512]{2,1,0:T(8,128)(2,1)}), bf16[16,32,512]{2,1,0:T(8,128)(2,1)S(1)}, u32[]{:S(2)}, u32[]{:S(2)}) async-start(bf16[16,32,512]{2,1,0:T(8,128)(2,1)} %bitcast.9), calls=%async_computation | async-start | bytes 1048576 | tf_op jit(solution)/shard_map/all_to_all | solution.py:143
  43.0 0.1 select_reduce_fusion.index_ref
  43.1 9.9 %all-to-all-done.x_ref = bf16[16,32,512]{2,1,0:T(8,128)(2,1)S(1)} async-done(((bf16[16,32,512]{2,1,0:T(8,128)(2,1)}), bf16[16,32,512]{2,1,0:T(8,128)(2,1)S(1)}, u32[]{:S(2)}, u32[]{:S(2)}) %all-to-all-start) | async-done | bytes 524320 | tf_op jit(solution)/shard_map/all_to_all | solution.py:143
  53.0 0.7 pick.2
  53.7 17.4 %all_to_all.20.g_ref = bf16[16,2,32,512]{3,2,1,0:T(8,128)(2,1)S(1)} all-to-all(bf16[16,2,32,512]{3,2,1,0:T(8,128)(2,1)S(1)} %bitcast.46), channel_id=1, replica_groups=mesh['replica'=8,'fsdp'=16] {'fsdp'}, dimensions={0} | all-to-all | bytes 2097152 | tf_op jit(solution)/shard_map/all_to_all | solution.py:145
  71.1 5.2 %slot_step.1 = (bf16[2,512,512]{2,1,0:T(8,128)(2,1)}, f32[2,512,512]{2,1,0:T(8,128)}, bf16[16,2,32,512]{3,2,1,0:T(8,128)(2,1)S(1)}) custom-call(bf16[16,2,32,512]{3,2,1,0:T(8,128)(2,1)S(1)} %all_to_all.20.g_ref, bf16[2,2,512,512]{3,2,1,0:T(8,128)(2,1)S(1)} %bitcast.48, bf16[2,512,512]{2,1,0:T(8,128)(2,1)S(1)} %bitcast.49, f32[2,512,512]{2,1,0:T(8,128)} %bitcast.54), custom_call_target="tpu_custom_call" | custom-call | tf_op jit(solution)/shard_map/slot_step/pallas_call | solution.py:93
  76.3 16.0 %all_to_all.21 = bf16[16,2,32,512]{3,2,1,0:T(8,128)(2,1)S(1)} all-to-all(bf16[16,2,32,512]{3,2,1,0:T(8,128)(2,1)S(1)} %get-tuple-element.6), channel_id=1, replica_groups=mesh['replica'=8,'fsdp'=16] {'fsdp'}, dimensions={0} | all-to-all | bytes 2097152 | tf_op jit(solution)/shard_map/all_to_all | solution.py:151
  92.4 0.6 pick.3
  93.0 12.0 %all_to_all.22 = bf16[16,32,512]{2,1,0:T(8,128)(2,1)S(1)} all-to-all(bf16[16,32,512]{2,1,0:T(8,128)(2,1)S(1)} %pick.3), channel_id=1, replica_groups=mesh['replica'=8,'fsdp'=16] {'fsdp'}, dimensions={0} | all-to-all | bytes 1048576 | tf_op jit(solution)/shard_map/all_to_all | solution.py:153
  105.0 1.0 collective-permute-start.7
  106.0 0.1 collective-permute-start.9
  106.0 2.6 %collective-permute-start.11 = (bf16[256,512]{1,0:T(8,128)(2,1)S(1)}, bf16[256,512]{1,0:T(8,128)(2,1)S(1)}, u32[]{:S(2)}, u32[]{:S(2)}) collective-permute-start(bf16[256,512]{1,0:T(8,128)(2,1)S(1)} %bitcast.58), channel_id=1, source_target_pairs={{0,96},{16,112},{32,0},{48,16},{64,32},{80,48},{96,64},{112,80},{1... | collective-permute-start | bytes 786440 | tf_op jit(solution)/shard_map/ppermute | solution.py:119
  108.6 0.6 collective-permute-start.13
  109.2 2.3 %collective-permute-done.7 = bf16[256,512]{1,0:T(8,128)(2,1)S(1)} collective-permute-done((bf16[256,512]{1,0:T(8,128)(2,1)S(1)}, bf16[256,512]{1,0:T(8,128)(2,1)S(1)}, u32[]{:S(2)}, u32[]{:S(2)}) %collective-permute-start.7) | collective-permute-done | bytes 262176 | tf_op jit(solution)/shard_map/ppermute | solution.py:116
  111.5 7.0 %collective-permute-start.8 = (bf16[256,512]{1,0:T(8,128)(2,1)S(1)}, bf16[256,512]{1,0:T(8,128)(2,1)S(1)}, u32[]{:S(2)}, u32[]{:S(2)}) collective-permute-start(bf16[256,512]{1,0:T(8,128)(2,1)S(1)} %collective-permute-done.7), channel_id=1, source_target_pairs={{0,16},{16,0},{32,48},{48,32},{64,80},{80,64},{96,112},{112,96},{1... | collective-permute-start | bytes 786440 | tf_op jit(solution)/shard_map/ppermute | solution.py:126
  118.5 2.8 %collective-permute-start.10 = (bf16[256,512]{1,0:T(8,128)(2,1)S(1)}, bf16[256,512]{1,0:T(8,128)(2,1)S(1)}, u32[]{:S(2)}, u32[]{:S(2)}) collective-permute-start(bf16[256,512]{1,0:T(8,128)(2,1)S(1)} %collective-permute-done.9), channel_id=1, source_target_pairs={{0,16},{16,0},{32,48},{48,32},{64,80},{80,64},{96,112},{112,96},{1... | collective-permute-start | bytes 786440 | tf_op jit(solution)/shard_map/ppermute | solution.py:126
  121.3 0.5 broadcast_in_dim.23
  121.8 0.1 collective-permute-start.19
  121.9 0.5 collective-permute-start.12
  122.4 0.1 collective-permute-start.14
  122.6 2.5 %collective-permute-start.17 = (bf16[256,512]{1,0:T(8,128)(2,1)S(1)}, bf16[256,512]{1,0:T(8,128)(2,1)S(1)}, u32[]{:S(2)}, u32[]{:S(2)}) collective-permute-start(bf16[256,512]{1,0:T(8,128)(2,1)S(1)} %collective-permute-done.13), channel_id=1, source_target_pairs={{0,96},{16,112},{32,0},{48,16},{64,32},{80,48},{96,64},{112,80},{1... | collective-permute-start | bytes 786440 | tf_op jit(solution)/shard_map/ppermute | solution.py:121
  125.1 2.5 %collective-permute-done.15 = bf16[256,512]{1,0:T(8,128)(2,1)S(1)} collective-permute-done((bf16[256,512]{1,0:T(8,128)(2,1)S(1)}, bf16[256,512]{1,0:T(8,128)(2,1)S(1)}, u32[]{:S(2)}, u32[]{:S(2)}) %collective-permute-start.15) | collective-permute-done | bytes 262176 | tf_op jit(solution)/shard_map/ppermute | solution.py:120
  127.6 0.8 collective-permute-start.16
  128.5 1.7 %collective-permute-done.17 = bf16[256,512]{1,0:T(8,128)(2,1)S(1)} collective-permute-done((bf16[256,512]{1,0:T(8,128)(2,1)S(1)}, bf16[256,512]{1,0:T(8,128)(2,1)S(1)}, u32[]{:S(2)}, u32[]{:S(2)}) %collective-permute-start.17) | collective-permute-done | bytes 262176 | tf_op jit(solution)/shard_map/ppermute | solution.py:121
  130.2 1.4 %collective-permute-start.18 = (bf16[256,512]{1,0:T(8,128)(2,1)S(1)}, bf16[256,512]{1,0:T(8,128)(2,1)S(1)}, u32[]{:S(2)}, u32[]{:S(2)}) collective-permute-start(bf16[256,512]{1,0:T(8,128)(2,1)S(1)} %collective-permute-done.17), channel_id=1, source_target_pairs={{0,16},{16,0},{32,48},{48,32},{64,80},{80,64},{96,112},{112,96},{1... | collective-permute-start | bytes 786440 | tf_op jit(solution)/shard_map/ppermute | solution.py:126
  131.8 1.0 collective-permute-done.18
  132.8 0.1 constant_dynamic-update-slice_fusion.1
  132.9 0.1 constant_dynamic-update-slice_fusion
  133.0 2.0 %copy-done.3 = bf16[512,4096]{1,0:T(8,128)(2,1)} copy-done((bf16[512,4096]{1,0:T(8,128)(2,1)}, bf16[512,4096]{1,0:T(8,128)(2,1)S(1)}, u32[]{:S(2)}) %copy-start.3) | copy-done | bytes 4194328
  (35 shorter events, 0.5 us)
Async XLA Ops:
  4.0 5.4 %collective-permute-start = (bf16[4,512,512]{2,1,0:T(8,128)(2,1)}, bf16[4,512,512]{2,1,0:T(8,128)(2,1)S(1)}, u32[]{:S(2)}, u32[]{:S(2)}) collective-permute-start(bf16[4,512,512]{2,1,0:T(8,128)(2,1)} %pad_maximum_fusion), channel_id=1, source_target_pairs={{0,16},{16,0},{32,48},{48,32},{64,80},{80,64},{96,112},{112,96},{1... | collective-permute-start | bytes 6291464 | tf_op jit(solution)/shard_map/ppermute | solution.py:35
  11.5 31.5 %copy-start.2 = (s32[16,1]{0,1:T(1,128)S(1)}, s32[16,1]{0,1:T(1,128)}, u32[]{:S(2)}) copy-start(s32[16,1]{0,1:T(1,128)} %param.6) | copy-start | bytes 196
  11.6 9.2 %collective-permute-start.5 = (bf16[256,512]{1,0:T(8,128)(2,1)S(1)}, bf16[256,512]{1,0:T(8,128)(2,1)S(1)}, u32[]{:S(2)}, u32[]{:S(2)}) collective-permute-start(bf16[256,512]{1,0:T(8,128)(2,1)S(1)} %get-tuple-element.22), channel_id=1, source_target_pairs={{0,96},{16,112},{32,0},{48,16},{64,32},{80,48},{96,64},{112,80},{1... | collective-permute-start | bytes 786440 | tf_op jit(solution)/shard_map/ppermute | solution.py:38
  15.5 8.9 %collective-permute-start.2 = (bf16[256,512]{1,0:T(8,128)(2,1)S(1)}, bf16[256,512]{1,0:T(8,128)(2,1)S(1)}, u32[]{:S(2)}, u32[]{:S(2)}) collective-permute-start(bf16[256,512]{1,0:T(8,128)(2,1)S(1)} %get-tuple-element.21), channel_id=1, source_target_pairs={{0,32},{16,48},{32,64},{48,80},{64,96},{80,112},{96,0},{112,16},{1... | collective-permute-start | bytes 786440 | tf_op jit(solution)/shard_map/ppermute | solution.py:37
  15.5 10.9 %collective-permute-start.1 = (bf16[256,512]{1,0:T(8,128)(2,1)S(1)}, bf16[256,512]{1,0:T(8,128)(2,1)S(1)}, u32[]{:S(2)}, u32[]{:S(2)}) collective-permute-start(bf16[256,512]{1,0:T(8,128)(2,1)S(1)} %slice_bitcast_fusion.7), channel_id=1, source_target_pairs={{0,96},{16,112},{32,0},{48,16},{64,32},{80,48},{96,64},{112,80},{1... | collective-permute-start | bytes 786440 | tf_op jit(solution)/shard_map/ppermute | solution.py:40
  18.3 11.3 %collective-permute-start.4 = (bf16[256,512]{1,0:T(8,128)(2,1)S(1)}, bf16[256,512]{1,0:T(8,128)(2,1)S(1)}, u32[]{:S(2)}, u32[]{:S(2)}) collective-permute-start(bf16[256,512]{1,0:T(8,128)(2,1)S(1)} %slice_bitcast_fusion.4), channel_id=1, source_target_pairs={{0,32},{16,48},{32,64},{48,80},{64,96},{80,112},{96,0},{112,16},{1... | collective-permute-start | bytes 786440 | tf_op jit(solution)/shard_map/ppermute | solution.py:39
  20.9 11.2 %collective-permute-start.6 = (bf16[256,512]{1,0:T(8,128)(2,1)S(1)}, bf16[256,512]{1,0:T(8,128)(2,1)S(1)}, u32[]{:S(2)}, u32[]{:S(2)}) collective-permute-start(bf16[256,512]{1,0:T(8,128)(2,1)S(1)} %fusion.7), channel_id=1, source_target_pairs={{0,96},{16,112},{32,0},{48,16},{64,32},{80,48},{96,64},{112,80},{1... | collective-permute-start | bytes 786440 | tf_op jit(solution)/shard_map/ppermute | solution.py:42
  24.4 10.7 %collective-permute-start.3 = (bf16[256,512]{1,0:T(8,128)(2,1)S(1)}, bf16[256,512]{1,0:T(8,128)(2,1)S(1)}, u32[]{:S(2)}, u32[]{:S(2)}) collective-permute-start(bf16[256,512]{1,0:T(8,128)(2,1)S(1)} %fusion.8), channel_id=1, source_target_pairs={{0,32},{16,48},{32,64},{48,80},{64,96},{80,112},{96,0},{112,16},{1... | collective-permute-start | bytes 786440 | tf_op jit(solution)/shard_map/ppermute | solution.py:41
  35.1 36.0 %copy-start = (bf16[1,1,2,2,512,512]{5,4,3,2,1,0:T(8,128)(2,1)S(1)}, bf16[1,1,2,2,512,512]{5,4,3,2,1,0:T(8,128)(2,1)}, u32[]{:S(2)}) copy-start(bf16[1,1,2,2,512,512]{5,4,3,2,1,0:T(8,128)(2,1)} %param.7) | copy-start | bytes 6291460
  36.2 16.7 %all-to-all-start = ((bf16[16,32,512]{2,1,0:T(8,128)(2,1)}), bf16[16,32,512]{2,1,0:T(8,128)(2,1)S(1)}, u32[]{:S(2)}, u32[]{:S(2)}) async-start(bf16[16,32,512]{2,1,0:T(8,128)(2,1)} %bitcast.9), calls=%async_computation | async-start | bytes 1048576 | tf_op jit(solution)/shard_map/all_to_all | solution.py:143
  53.0 18.1 %copy-start.1 = (bf16[1,1,2,512,512]{4,3,2,1,0:T(8,128)(2,1)S(1)}, bf16[1,1,2,512,512]{4,3,2,1,0:T(8,128)(2,1)}, u32[]{:S(2)}) copy-start(bf16[1,1,2,512,512]{4,3,2,1,0:T(8,128)(2,1)} %param.8) | copy-start | bytes 3145732
  105.0 6.5 %collective-permute-start.7 = (bf16[256,512]{1,0:T(8,128)(2,1)S(1)}, bf16[256,512]{1,0:T(8,128)(2,1)S(1)}, u32[]{:S(2)}, u32[]{:S(2)}) collective-permute-start(bf16[256,512]{1,0:T(8,128)(2,1)S(1)} %bitcast.57), channel_id=1, source_target_pairs={{0,32},{16,48},{32,64},{48,80},{64,96},{80,112},{96,0},{112,16},{1... | collective-permute-start | bytes 786440 | tf_op jit(solution)/shard_map/ppermute | solution.py:116
  106.0 12.5 %collective-permute-start.9 = (bf16[256,512]{1,0:T(8,128)(2,1)S(1)}, bf16[256,512]{1,0:T(8,128)(2,1)S(1)}, u32[]{:S(2)}, u32[]{:S(2)}) collective-permute-start(bf16[256,512]{1,0:T(8,128)(2,1)S(1)} %bitcast.55), channel_id=1, source_target_pairs={{0,32},{16,48},{32,64},{48,80},{64,96},{80,112},{96,0},{112,16},{1... | collective-permute-start | bytes 786440 | tf_op jit(solution)/shard_map/ppermute | solution.py:118
  106.0 15.8 %collective-permute-start.11 = (bf16[256,512]{1,0:T(8,128)(2,1)S(1)}, bf16[256,512]{1,0:T(8,128)(2,1)S(1)}, u32[]{:S(2)}, u32[]{:S(2)}) collective-permute-start(bf16[256,512]{1,0:T(8,128)(2,1)S(1)} %bitcast.58), channel_id=1, source_target_pairs={{0,96},{16,112},{32,0},{48,16},{64,32},{80,48},{96,64},{112,80},{1... | collective-permute-start | bytes 786440 | tf_op jit(solution)/shard_map/ppermute | solution.py:119
  108.6 13.3 %collective-permute-start.13 = (bf16[256,512]{1,0:T(8,128)(2,1)S(1)}, bf16[256,512]{1,0:T(8,128)(2,1)S(1)}, u32[]{:S(2)}, u32[]{:S(2)}) collective-permute-start(bf16[256,512]{1,0:T(8,128)(2,1)S(1)} %bitcast.56), channel_id=1, source_target_pairs={{0,96},{16,112},{32,0},{48,16},{64,32},{80,48},{96,64},{112,80},{1... | collective-permute-start | bytes 786440 | tf_op jit(solution)/shard_map/ppermute | solution.py:117
  111.5 10.9 %collective-permute-start.8 = (bf16[256,512]{1,0:T(8,128)(2,1)S(1)}, bf16[256,512]{1,0:T(8,128)(2,1)S(1)}, u32[]{:S(2)}, u32[]{:S(2)}) collective-permute-start(bf16[256,512]{1,0:T(8,128)(2,1)S(1)} %collective-permute-done.7), channel_id=1, source_target_pairs={{0,16},{16,0},{32,48},{48,32},{64,80},{80,64},{96,112},{112,96},{1... | collective-permute-start | bytes 786440 | tf_op jit(solution)/shard_map/ppermute | solution.py:126
  118.5 9.1 %collective-permute-start.15 = (bf16[256,512]{1,0:T(8,128)(2,1)S(1)}, bf16[256,512]{1,0:T(8,128)(2,1)S(1)}, u32[]{:S(2)}, u32[]{:S(2)}) collective-permute-start(bf16[256,512]{1,0:T(8,128)(2,1)S(1)} %collective-permute-done.7), channel_id=1, source_target_pairs={{0,32},{16,48},{32,64},{48,80},{64,96},{80,112},{96,0},{112,16},{1... | collective-permute-start | bytes 786440 | tf_op jit(solution)/shard_map/ppermute | solution.py:120
  118.5 4.1 %collective-permute-start.10 = (bf16[256,512]{1,0:T(8,128)(2,1)S(1)}, bf16[256,512]{1,0:T(8,128)(2,1)S(1)}, u32[]{:S(2)}, u32[]{:S(2)}) collective-permute-start(bf16[256,512]{1,0:T(8,128)(2,1)S(1)} %collective-permute-done.9), channel_id=1, source_target_pairs={{0,16},{16,0},{32,48},{48,32},{64,80},{80,64},{96,112},{112,96},{1... | collective-permute-start | bytes 786440 | tf_op jit(solution)/shard_map/ppermute | solution.py:126
  121.8 11.1 %collective-permute-start.19 = (bf16[512,512]{1,0:T(8,128)(2,1)S(1)}, bf16[512,512]{1,0:T(8,128)(2,1)S(1)}, u32[]{:S(2)}, u32[]{:S(2)}) collective-permute-start(bf16[512,512]{1,0:T(8,128)(2,1)S(1)} %bitcast.52), channel_id=1, source_target_pairs={{0,16},{16,0},{32,48},{48,32},{64,80},{80,64},{96,112},{112,96},{1... | collective-permute-start | bytes 1572872 | tf_op jit(solution)/shard_map/ppermute | solution.py:115
  121.9 6.5 %collective-permute-start.12 = (bf16[256,512]{1,0:T(8,128)(2,1)S(1)}, bf16[256,512]{1,0:T(8,128)(2,1)S(1)}, u32[]{:S(2)}, u32[]{:S(2)}) collective-permute-start(bf16[256,512]{1,0:T(8,128)(2,1)S(1)} %collective-permute-done.11), channel_id=1, source_target_pairs={{0,16},{16,0},{32,48},{48,32},{64,80},{80,64},{96,112},{112,96},{1... | collective-permute-start | bytes 786440 | tf_op jit(solution)/shard_map/ppermute | solution.py:126
  122.4 9.2 %collective-permute-start.14 = (bf16[256,512]{1,0:T(8,128)(2,1)S(1)}, bf16[256,512]{1,0:T(8,128)(2,1)S(1)}, u32[]{:S(2)}, u32[]{:S(2)}) collective-permute-start(bf16[256,512]{1,0:T(8,128)(2,1)S(1)} %collective-permute-done.13), channel_id=1, source_target_pairs={{0,16},{16,0},{32,48},{48,32},{64,80},{80,64},{96,112},{112,96},{1... | collective-permute-start | bytes 786440 | tf_op jit(solution)/shard_map/ppermute | solution.py:126
  122.6 7.6 %collective-permute-start.17 = (bf16[256,512]{1,0:T(8,128)(2,1)S(1)}, bf16[256,512]{1,0:T(8,128)(2,1)S(1)}, u32[]{:S(2)}, u32[]{:S(2)}) collective-permute-start(bf16[256,512]{1,0:T(8,128)(2,1)S(1)} %collective-permute-done.13), channel_id=1, source_target_pairs={{0,96},{16,112},{32,0},{48,16},{64,32},{80,48},{96,64},{112,80},{1... | collective-permute-start | bytes 786440 | tf_op jit(solution)/shard_map/ppermute | solution.py:121
  127.6 4.1 %collective-permute-start.16 = (bf16[256,512]{1,0:T(8,128)(2,1)S(1)}, bf16[256,512]{1,0:T(8,128)(2,1)S(1)}, u32[]{:S(2)}, u32[]{:S(2)}) collective-permute-start(bf16[256,512]{1,0:T(8,128)(2,1)S(1)} %collective-permute-done.15), channel_id=1, source_target_pairs={{0,16},{16,0},{32,48},{48,32},{64,80},{80,64},{96,112},{112,96},{1... | collective-permute-start | bytes 786440 | tf_op jit(solution)/shard_map/ppermute | solution.py:126
  130.2 2.5 %collective-permute-start.18 = (bf16[256,512]{1,0:T(8,128)(2,1)S(1)}, bf16[256,512]{1,0:T(8,128)(2,1)S(1)}, u32[]{:S(2)}, u32[]{:S(2)}) collective-permute-start(bf16[256,512]{1,0:T(8,128)(2,1)S(1)} %collective-permute-done.17), channel_id=1, source_target_pairs={{0,16},{16,0},{32,48},{48,32},{64,80},{80,64},{96,112},{112,96},{1... | collective-permute-start | bytes 786440 | tf_op jit(solution)/shard_map/ppermute | solution.py:126
  132.9 2.0 %copy-start.3 = (bf16[512,4096]{1,0:T(8,128)(2,1)}, bf16[512,4096]{1,0:T(8,128)(2,1)S(1)}, u32[]{:S(2)}) copy-start(bf16[512,4096]{1,0:T(8,128)(2,1)S(1)} %constant_dynamic-update-slice_fusion) | copy-start | bytes 12582916

commit v2 on v1

v2 whole, which is shorter than its diff:
```python
import jax
import jax.numpy as jnp
from jax import lax
from jax.experimental import pallas as pl
from jax.experimental.pallas import tpu as pltpu
from jax.sharding import PartitionSpec as P

SIDE = 512
SLOTS = 2
PEERS = 16
PIECE = SIDE // PEERS
HALF = SIDE // 2
VMEM_LIMIT = 24 * 1024 * 1024


def ring(step):
    return [(i, ((i // 2 + step) % 4) * 2 + i % 2) for i in range(8)]


UP = ring(1)
DOWN = ring(3)
CORES = [(i, i ^ 1) for i in range(8)]


def add(a, b):
    return (a.astype(jnp.float32) + b.astype(jnp.float32)).astype(jnp.bfloat16)


def vmem_call(kernel, name, out_shape, *operands):
    spec = pl.BlockSpec(memory_space=pltpu.VMEM)
    return pl.pallas_call(
        kernel,
        out_shape=out_shape,
        in_specs=[spec] * len(operands),
        out_specs=jax.tree.map(lambda _: spec, out_shape),
        compiler_params=pltpu.CompilerParams(vmem_limit_bytes=VMEM_LIMIT),
        name=name,
    )(*operands)


def swap(x):
    with jax.named_scope("swap"):
        return lax.ppermute(x, "replica", CORES)


def up(x, name):
    with jax.named_scope(name):
        return lax.ppermute(x, "replica", UP)


def down(x, name):
    with jax.named_scope(name):
        return lax.ppermute(x, "replica", DOWN)


def home_kernel(a_ref, t1_ref, t2_ref, l1_ref, l2_ref, o_ref):
    for n, (x_ref, y_ref) in enumerate(((t1_ref, t2_ref), (l1_ref, l2_ref))):
        rows = pl.ds(n * HALF, HALF)
        total = a_ref[rows] + x_ref[...].astype(jnp.float32) + y_ref[...].astype(jnp.float32)
        o_ref[rows] = total.astype(jnp.bfloat16)


def sum_replicas(grads, z, core, extra):
    def part(x, d, which):
        col = (lax.rem(z + d, 4) * 2 + which) * SIDE
        return lax.dynamic_slice(x, (0, col), (SIDE, SIDE))

    def halves(x):
        x = x.astype(jnp.bfloat16)
        return x[:HALF], x[HALF:]

    def both(x, d, got):
        return part(x, d, core).astype(jnp.float32) + got.astype(jnp.float32)

    give2 = part(grads, 2, 1 - core)
    later, give2 = lax.optimization_barrier((grads, give2))
    got2 = swap(give2)
    got1, got3, got0 = (swap(part(later, d, 1 - core)) for d in (1, 3, 0))
    s2 = both(later, 2, got2).astype(jnp.bfloat16)
    later, s2, extra = lax.optimization_barrier((later, s2, extra))
    top2, low2 = halves(s2)
    up1, down1 = up(top2, "up1"), down(low2, "down1")
    top1, low1 = halves(both(later, 1, got1))
    top3, low3 = halves(both(later, 3, got3))
    up2, down2 = up(low1, "up2"), down(top3, "down2")
    up3, down3 = up(add(top1, up1), "up3"), down(add(low3, down1), "down3")
    shape = jax.ShapeDtypeStruct((SIDE, SIDE), jnp.bfloat16)
    home = vmem_call(home_kernel, "home", shape, both(later, 0, got0), down2, up3, up2, down3)
    return home, extra


def pick_kernel(index_ref, x_ref, o_ref):
    for t in range(o_ref.shape[0]):
        i = index_ref[t]
        v = x_ref[jnp.maximum(i, 0)]
        o_ref[t] = jnp.where(i >= 0, v, jnp.zeros_like(v))


def pick(index, x, count):
    return pl.pallas_call(
        pick_kernel,
        out_shape=jax.ShapeDtypeStruct((count,) + x.shape[1:], x.dtype),
        in_specs=[
            pl.BlockSpec(memory_space=pltpu.SMEM),
            pl.BlockSpec(memory_space=pltpu.VMEM),
        ],
        out_specs=pl.BlockSpec(memory_space=pltpu.VMEM),
        compiler_params=pltpu.CompilerParams(vmem_limit_bytes=VMEM_LIMIT),
        name="pick",
    )(index, x)


def tile_sum(x):
    return jnp.sum(x.reshape(-1, 8, SIDE), axis=0)


def slot_kernel(
    g_ref, f_ref, m_ref, a_hbm, mo_hbm, ao_hbm, u_ref,
    a_ref, ao_ref, mo_ref, p_ref, i_ref, a_sem, ao_sem, mo_sem,
):
    slots = range(SLOTS)
    a_in = [pltpu.make_async_copy(a_hbm.at[s], a_ref.at[s], a_sem.at[s]) for s in slots]
    a_out = [pltpu.make_async_copy(ao_ref.at[s], ao_hbm.at[s], ao_sem.at[s]) for s in slots]
    m_out = [pltpu.make_async_copy(mo_ref.at[s], mo_hbm.at[s], mo_sem.at[s]) for s in slots]
    for s in slots:
        a_in[s].start()
    for s in slots:
        g = g_ref[:, s].reshape(SIDE, SIDE)
        inner = jnp.dot(f_ref[s, 0], g, preferred_element_type=jnp.float32)
        i_ref[s] = inner.astype(jnp.bfloat16)
    for s in slots:
        p_ref[s] = jnp.dot(i_ref[s], f_ref[s, 1], preferred_element_type=jnp.float32)
    ratio = []
    for s in slots:
        a_in[s].wait()
        adagrad = norm = jnp.zeros((8, SIDE), jnp.float32)
        for k in range(PEERS):
            rows = pl.ds(k * PIECE, PIECE)
            g = g_ref[k, s].astype(jnp.float32)
            squares = g * g
            accum = a_ref[s, rows] + squares
            ao_ref[s, rows] = accum
            adagrad += tile_sum(squares / accum)
            precond = p_ref[s, rows]
            norm += tile_sum(precond * precond)
        a_out[s].start()
        ratio.append(jnp.sqrt(jnp.sum(adagrad)) / jnp.sqrt(jnp.sum(norm) + 1e-06))
    for s in slots:
        for k in range(PEERS):
            rows = pl.ds(k * PIECE, PIECE)
            step = p_ref[s, rows] * ratio[s]
            moment = (0.9 * m_ref[s, rows].astype(jnp.float32) + step).astype(jnp.bfloat16)
            mo_ref[s, rows] = moment
            u_ref[k, s] = (0.9 * moment.astype(jnp.float32) + step).astype(jnp.bfloat16)
        m_out[s].start()
    for c in a_out + m_out:
        c.wait()


def slot_step(g, factors, momentum, accum):
    vmem, hbm = pl.BlockSpec(memory_space=pltpu.VMEM), pl.BlockSpec(memory_space=pltpu.HBM)
    slots = (SLOTS, SIDE, SIDE)
    return pl.pallas_call(
        slot_kernel,
        out_shape=(
            jax.ShapeDtypeStruct(slots, jnp.bfloat16),
            jax.ShapeDtypeStruct(slots, jnp.float32),
            jax.ShapeDtypeStruct(g.shape, jnp.bfloat16),
        ),
        in_specs=[vmem, vmem, vmem, hbm],
        out_specs=(hbm, hbm, vmem),
        scratch_shapes=[
            pltpu.VMEM(slots, jnp.float32),
            pltpu.VMEM(slots, jnp.float32),
            pltpu.VMEM(slots, jnp.bfloat16),
            pltpu.VMEM(slots, jnp.float32),
            pltpu.VMEM(slots, jnp.bfloat16),
            pltpu.SemaphoreType.DMA((SLOTS,)),
            pltpu.SemaphoreType.DMA((SLOTS,)),
            pltpu.SemaphoreType.DMA((SLOTS,)),
        ],
        compiler_params=pltpu.CompilerParams(vmem_limit_bytes=VMEM_LIMIT),
        name="slot_step",
    )(g, factors, momentum, accum)


def gather_replicas(tile, z, core):
    up1, down1 = up(tile[:HALF], "up1"), down(tile[HALF:], "down1")
    tile, own = lax.optimization_barrier((tile, swap(tile)))
    up2, down2 = up(tile[HALF:], "up2"), down(tile[:HALF], "down2")
    up3, down3 = up(up1, "up3"), down(down1, "down3")
    near = lax.optimization_barrier((up1, up2, down2, down1))
    other = [swap(x) for x in near]
    up3, down3, *other = lax.optimization_barrier((up3, down3, *other))
    out = jnp.zeros((SIDE, 8 * SIDE), tile.dtype)

    def put(out, x, row, d, which):
        return lax.dynamic_update_slice(out, x, (row, (lax.rem(z + d, 4) * 2 + which) * SIDE))

    out = put(put(out, tile, 0, 0, core), own, 0, 0, 1 - core)
    halves = [*zip(near, other), (up3, swap(up3)), (down3, swap(down3))]
    for n, (x, y) in enumerate(halves):
        row, d = n % 2 * HALF, (3, 1, 2)[n // 2]
        out = put(put(out, x, row, d, core), y, row, d, 1 - core)
    return out


def body(grads, owners, factors, momentum, accum):
    replica = lax.axis_index("replica")
    z, core = replica // 2, lax.rem(replica, 2)
    ids = owners[:, 0]
    named = ids[None, :] == jnp.arange(PEERS * SLOTS, dtype=jnp.int32)[:, None]
    block_of = jnp.max(
        jnp.where(named, jnp.arange(PEERS, dtype=jnp.int32)[None, :], -1), axis=1
    )

    home, block_of = sum_replicas(grads[0], z, core, block_of)
    pieces = lax.all_to_all(home.reshape(PEERS, PIECE, SIDE), "fsdp", 0, 0, tiled=True)
    routed = pick(block_of, pieces, PEERS * SLOTS)
    slot_grad = lax.all_to_all(
        routed.reshape(PEERS, SLOTS, PIECE, SIDE), "fsdp", 0, 0, tiled=True
    )
    moment_new, squares_new, update = slot_step(
        slot_grad, factors[0, 0], momentum[0, 0], accum[0, 0]
    )
    back = lax.all_to_all(update, "fsdp", 0, 0, tiled=True)
    back = pick(ids, back.reshape(PEERS * SLOTS, PIECE, SIDE), PEERS)
    tile = lax.all_to_all(back, "fsdp", 0, 0, tiled=True).reshape(SIDE, SIDE)
    out = gather_replicas(tile, z, core)
    return (out, moment_new[None, None], squares_new[None, None])


def solution(mesh):
    in_specs = (
        P("replica", "fsdp", None),
        P(None, "replica"),
        P("replica", "fsdp", None, None, None, None),
        P("replica", "fsdp", None, None, None),
        P("replica", "fsdp", None, None, None),
    )
    out_specs = (
        P("fsdp", None),
        P("replica", "fsdp", None, None, None),
        P("replica", "fsdp", None, None, None),
    )
    return jax.shard_map(body, mesh=mesh, in_specs=in_specs, out_specs=out_specs, check_vma=False)
```

time: 135 us -> 130 us (0.963)
  blocking collectives: 45.4 us -> 59.8 us
  waiting for transfers between devices: 34.5 us -> 23.1 us
  starting transfers between devices: 37.8 us -> 30.9 us
  other arithmetic: 5.02 us -> 3.3 us
  local copies, waits for them, and re-layouts: 4.75 us -> 6.47 us
    all_to_all x0 -> x1, blocking collectives: none -> 15.9 us  [body(): lax.all_to_all(home.reshape(PEERS, PIECE, SIDE), 'fsdp', 0, 0, tiled=True)]
    all_to_all x1 -> x0, waiting for transfers between devices: 9.89 us -> none  [body(): lax.all_to_all(home.reshape(PEERS, PIECE, SIDE), 'fsdp', 0, 0, tiled=True)]
    all_to_all x1 -> x0, starting transfers between devices: 6.75 us -> none  [body(): lax.all_to_all(home.reshape(PEERS, PIECE, SIDE), 'fsdp', 0, 0, tiled=True)]
    convert_element_type x0 -> x2, other arithmetic: none -> 3.07 us  [the longest x1 1.73 us: halves(): x = x.astype(jnp.bfloat16)]
    convert_element_type x3 -> x2, other arithmetic: 2.25 us -> 0.14 us  [add(): return (a.astype(jnp.float32) + b.astype(jnp.float32)).astype(jnp.bfloat16)]
    another operation x2 -> x0, other arithmetic: 1.86 us -> none  [the longest x1 1.58 us: sum_replicas(): give = jnp.stack([part(d, 1 - core) for d in (2, 1, 3, 0)])]
    dynamic_slice x1 -> x2, local copies, waits for them, and re-layouts: 1.67 us -> 3.34 us  [part(): return lax.dynamic_slice(x, (0, col), (SIDE, SIDE))]
    ppermute x20 -> x23, waiting for transfers between devices: 24.6 us -> 23.1 us  [the longest x6 19.7 us: up(): return lax.ppermute(x, 'replica', UP)]
  transfers between devices with their start and end apart: 21 -> 23, of which waited for: 11 -> 10; matrix products, arithmetic and copies ran while one was open for 1% -> 4% of each run, Pallas kernels for 0% -> 0%
where the time goes in v2:
time: 130 us
  blocking collectives  59.8 us (46%)
  starting transfers between devices  30.9 us (24%)
  waiting for transfers between devices  23.1 us (18%)
  local copies, waits for them, and re-layouts  6.47 us (5%)
  Pallas kernels  5.2 us (4%)
  other arithmetic  3.3 us (3%)
    ppermute x6, waiting for transfers between devices, up(): return lax.ppermute(x, 'replica', UP)  19.7 us
    all_to_all x1, blocking collectives, body(): back = lax.all_to_all(update, 'fsdp', 0, 0, tiled=True)  16.1 us
    all_to_all x1, blocking collectives, body(): lax.all_to_all(routed.reshape(PEERS, SLOTS, PIECE, SIDE), 'fsdp', 0, 0, t...  16 us
    all_to_all x1, blocking collectives, body(): lax.all_to_all(home.reshape(PEERS, PIECE, SIDE), 'fsdp', 0, 0, tiled=True)  15.9 us
    ppermute x6, starting transfers between devices, down(): return lax.ppermute(x, 'replica', DOWN)  15.7 us
    all_to_all x1, blocking collectives, body(): tile = lax.all_to_all(back, 'fsdp', 0, 0, tiled=True).reshape(SIDE, SIDE)  11.7 us
    ppermute x11, starting transfers between devices, swap(): return lax.ppermute(x, 'replica', CORES)  11.1 us
    ppermute x6, starting transfers between devices, up(): return lax.ppermute(x, 'replica', UP)  4.14 us
  transfers between devices with their start and end apart: 23, of which 10 were waited for; matrix products, arithmetic and copies ran while one was open for 4% of the time, Pallas kernels for 0%

profile of v2, /device:TPU:1, one launch (start us, length us, event | category | flops | bytes accessed | tf_op | source)
XLA Modules:
  0.0 129.8 jit_solution(1739856071910720522)
XLA Ops:
  0.7 1.9 %dynamic-slice_bitcast_fusion = bf16[512,512]{1,0:T(8,128)(2,1)} fusion(bf16[1,512,4096]{2,1,0:T(8,128)(2,1)} %param.5, s32[]{:T(128)S(6)} %select_n.48), kind=kLoop, calls=%fused_computation.6 | loop fusion | bytes 1048580 | tf_op jit(solution)/shard_map/dynamic_slice | solution.py:66
  2.5 1.4 %collective-permute-start = (bf16[512,512]{1,0:T(8,128)(2,1)}, bf16[512,512]{1,0:T(8,128)(2,1)}, u32[]{:S(2)}, u32[]{:S(2)}) collective-permute-start(bf16[512,512]{1,0:T(8,128)(2,1)} %dynamic-slice_bitcast_fusion), channel_id=1, source_target_pairs={{0,16},{16,0},{32,48},{48,32},{64,80},{80,64},{96,112},{112,96},{1... | collective-permute-start | bytes 1572872 | tf_op jit(solution)/shard_map/swap/ppermute | solution.py:43
  4.0 1.5 %constant_dynamic-slice_fusion = (bf16[512,512]{1,0:T(8,128)(2,1)S(1)}, bf16[512,512]{1,0:T(8,128)(2,1)S(1)}, bf16[512,512]{1,0:T(8,128)(2,1)S(1)}) fusion(bf16[512,4096]{1,0:T(8,128)(2,1)} %bitcast.26, s32[]{:T(128)S(6)} %select_n.56, s32[]{:T(128)S(6)} %select_n.54, s32[]{:T(128)S(6)} %select_n.52), kind=kLoop, calls=%fused_computation.17 | loop fusion | bytes 3145740 | tf_op jit(solution)/shard_map/dynamic_slice | solution.py:66
  5.4 0.1 collective-permute-start.4
  5.5 0.5 collective-permute-start.2
  6.0 0.1 collective-permute-start.1
  6.1 0.1 select_reduce_fusion.index_ref
  6.3 1.3 %add_convert_fusion.2 = bf16[512,512]{1,0:T(8,128)(2,1)S(1)} fusion(bf16[512,512]{1,0:T(8,128)(2,1)} %collective-permute-done, bf16[512,4096]{1,0:T(8,128)(2,1)} %bitcast.27, s32[]{:T(128)S(6)} %select_n.49), kind=kLoop, calls=%fused_computation.3 | loop fusion | flops 1048576 | bytes 1572868 | tf_op jit(solution)/shard_map/convert_element_type | solution.py:79
  7.6 1.8 %collective-permute-start.5 = (bf16[256,512]{1,0:T(8,128)(2,1)S(1)}, bf16[256,512]{1,0:T(8,128)(2,1)S(1)}, u32[]{:S(2)}, u32[]{:S(2)}) collective-permute-start(bf16[256,512]{1,0:T(8,128)(2,1)S(1)} %get-tuple-element.54), channel_id=1, source_target_pairs={{0,32},{16,48},{32,64},{48,80},{64,96},{80,112},{96,0},{112,16},{1... | collective-permute-start | bytes 786440 | tf_op jit(solution)/shard_map/up1/ppermute | solution.py:48
  9.4 2.2 %collective-permute-start.8 = (bf16[256,512]{1,0:T(8,128)(2,1)S(1)}, bf16[256,512]{1,0:T(8,128)(2,1)S(1)}, u32[]{:S(2)}, u32[]{:S(2)}) collective-permute-start(bf16[256,512]{1,0:T(8,128)(2,1)S(1)} %get-tuple-element.53), channel_id=1, source_target_pairs={{0,96},{16,112},{32,0},{48,16},{64,32},{80,48},{96,64},{112,80},{1... | collective-permute-start | bytes 786440 | tf_op jit(solution)/shard_map/down1/ppermute | solution.py:53
  11.6 1.7 %add_convert_fusion = (bf16[512,512]{1,0:T(8,128)(2,1)S(1)}, bf16[512,512]{1,0:T(8,128)(2,1)S(1)}, f32[512,512]{1,0:T(8,128)S(1)}) fusion(bf16[512,512]{1,0:T(8,128)(2,1)S(1)} %collective-permute-done.4, bf16[512,4096]{1,0:T(8,128)(2,1)} %bitcast.28, s32[]{:T(128)S(6)} %select_n.55, bf16[512,512]{1,0:T(8,128)(2,1)S(1)} %collective-permute-done.2, ...), kind=kLoop, calls=%fused_computation | loop fusion | flops 2883584 | bytes 5242892 | tf_op jit(solution)/shard_map/convert_element_type | solution.py:69
  13.4 1.5 %collective-permute-start.3 = (bf16[256,512]{1,0:T(8,128)(2,1)S(1)}, bf16[256,512]{1,0:T(8,128)(2,1)S(1)}, u32[]{:S(2)}, u32[]{:S(2)}) collective-permute-start(bf16[256,512]{1,0:T(8,128)(2,1)S(1)} %slice.48), channel_id=1, source_target_pairs={{0,96},{16,112},{32,0},{48,16},{64,32},{80,48},{96,64},{112,80},{1... | collective-permute-start | bytes 786440 | tf_op jit(solution)/shard_map/down2/ppermute | solution.py:53
  14.9 0.2 collective-permute-start.7
  15.0 2.8 %collective-permute-done.5 = bf16[256,512]{1,0:T(8,128)(2,1)S(1)} collective-permute-done((bf16[256,512]{1,0:T(8,128)(2,1)S(1)}, bf16[256,512]{1,0:T(8,128)(2,1)S(1)}, u32[]{:S(2)}, u32[]{:S(2)}) %collective-permute-start.5) | collective-permute-done | bytes 262176 | tf_op jit(solution)/shard_map/up1/ppermute | solution.py:48
  18.0 0.1 collective-permute-start.6
  18.1 0.1 add_convert_fusion.3
  18.2 2.7 %collective-permute-start.9 = (bf16[256,512]{1,0:T(8,128)(2,1)S(1)}, bf16[256,512]{1,0:T(8,128)(2,1)S(1)}, u32[]{:S(2)}, u32[]{:S(2)}) collective-permute-start(bf16[256,512]{1,0:T(8,128)(2,1)S(1)} %add_convert_fusion.3), channel_id=1, source_target_pairs={{0,96},{16,112},{32,0},{48,16},{64,32},{80,48},{96,64},{112,80},{1... | collective-permute-start | bytes 786440 | tf_op jit(solution)/shard_map/down3/ppermute | solution.py:53
  20.9 1.7 %collective-permute-done.3.t1_ref = bf16[256,512]{1,0:T(8,128)(2,1)S(1)} collective-permute-done((bf16[256,512]{1,0:T(8,128)(2,1)S(1)}, bf16[256,512]{1,0:T(8,128)(2,1)S(1)}, u32[]{:S(2)}, u32[]{:S(2)}) %collective-permute-start.3) | collective-permute-done | bytes 262176 | tf_op jit(solution)/shard_map/down2/ppermute | solution.py:53
  22.6 0.1 collective-permute-done.7.l1_ref
  22.7 5.6 %collective-permute-done.6.t2_ref = bf16[256,512]{1,0:T(8,128)(2,1)S(1)} collective-permute-done((bf16[256,512]{1,0:T(8,128)(2,1)S(1)}, bf16[256,512]{1,0:T(8,128)(2,1)S(1)}, u32[]{:S(2)}, u32[]{:S(2)}) %collective-permute-start.6) | collective-permute-done | bytes 262176 | tf_op jit(solution)/shard_map/up3/ppermute | solution.py:48
  28.3 0.2 home.1
  28.5 15.9 %all_to_all.20.x_ref = bf16[16,32,512]{2,1,0:T(8,128)(2,1)S(1)} all-to-all(bf16[16,32,512]{2,1,0:T(8,128)(2,1)S(1)} %bitcast.19), channel_id=1, replica_groups=mesh['replica'=8,'fsdp'=16] {'fsdp'}, dimensions={0} | all-to-all | bytes 1048576 | tf_op jit(solution)/shard_map/all_to_all | solution.py:218
  44.4 0.7 pick.2
  45.1 16.0 %all_to_all.21.g_ref = bf16[16,2,32,512]{3,2,1,0:T(8,128)(2,1)S(1)} all-to-all(bf16[16,2,32,512]{3,2,1,0:T(8,128)(2,1)S(1)} %bitcast.15), channel_id=1, replica_groups=mesh['replica'=8,'fsdp'=16] {'fsdp'}, dimensions={0} | all-to-all | bytes 2097152 | tf_op jit(solution)/shard_map/all_to_all | solution.py:220
  61.1 3.7 %slot_step.1 = (bf16[2,512,512]{2,1,0:T(8,128)(2,1)}, f32[2,512,512]{2,1,0:T(8,128)}, bf16[16,2,32,512]{3,2,1,0:T(8,128)(2,1)S(1)}) custom-call(bf16[16,2,32,512]{3,2,1,0:T(8,128)(2,1)S(1)} %all_to_all.21.g_ref, bf16[2,2,512,512]{3,2,1,0:T(8,128)(2,1)S(1)} %bitcast.17, bf16[2,512,512]{2,1,0:T(8,128)(2,1)S(1)} %bitcast.20, f32[2,512,512]{2,1,0:T(8,128)S(1)} %bitcast.18), custom_call_target="tpu_custom_call" | custom-call | tf_op jit(solution)/shard_map/slot_step/pallas_call | solution.py:163
  64.9 16.1 %all_to_all.22 = bf16[16,2,32,512]{3,2,1,0:T(8,128)(2,1)S(1)} all-to-all(bf16[16,2,32,512]{3,2,1,0:T(8,128)(2,1)S(1)} %get-tuple-element.28), channel_id=1, replica_groups=mesh['replica'=8,'fsdp'=16] {'fsdp'}, dimensions={0} | all-to-all | bytes 2097152 | tf_op jit(solution)/shard_map/all_to_all | solution.py:226
  81.0 0.6 pick.3
  81.6 11.7 %all_to_all.23 = bf16[16,32,512]{2,1,0:T(8,128)(2,1)S(1)} all-to-all(bf16[16,32,512]{2,1,0:T(8,128)(2,1)S(1)} %pick.3), channel_id=1, replica_groups=mesh['replica'=8,'fsdp'=16] {'fsdp'}, dimensions={0} | all-to-all | bytes 1048576 | tf_op jit(solution)/shard_map/all_to_all | solution.py:228
  93.4 6.5 %collective-permute-start.10 = (bf16[512,512]{1,0:T(8,128)(2,1)S(1)}, bf16[512,512]{1,0:T(8,128)(2,1)S(1)}, u32[]{:S(2)}, u32[]{:S(2)}) collective-permute-start(bf16[512,512]{1,0:T(8,128)(2,1)S(1)} %bitcast.23), channel_id=1, source_target_pairs={{0,16},{16,0},{32,48},{48,32},{64,80},{80,64},{96,112},{112,96},{1... | collective-permute-start | bytes 1572872 | tf_op jit(solution)/shard_map/swap/ppermute | solution.py:43
  99.9 2.0 %collective-permute-start.11 = (bf16[256,512]{1,0:T(8,128)(2,1)S(1)}, bf16[256,512]{1,0:T(8,128)(2,1)S(1)}, u32[]{:S(2)}, u32[]{:S(2)}) collective-permute-start(bf16[256,512]{1,0:T(8,128)(2,1)S(1)} %bitcast.30), channel_id=1, source_target_pairs={{0,32},{16,48},{32,64},{48,80},{64,96},{80,112},{96,0},{112,16},{1... | collective-permute-start | bytes 786440 | tf_op jit(solution)/shard_map/up1/ppermute | solution.py:48
  101.9 4.0 %collective-permute-start.14 = (bf16[256,512]{1,0:T(8,128)(2,1)S(1)}, bf16[256,512]{1,0:T(8,128)(2,1)S(1)}, u32[]{:S(2)}, u32[]{:S(2)}) collective-permute-start(bf16[256,512]{1,0:T(8,128)(2,1)S(1)} %bitcast.29), channel_id=1, source_target_pairs={{0,96},{16,112},{32,0},{48,16},{64,32},{80,48},{96,64},{112,80},{1... | collective-permute-start | bytes 786440 | tf_op jit(solution)/shard_map/down1/ppermute | solution.py:53
  106.0 0.1 collective-permute-start.12
  106.1 2.7 %collective-permute-start.13 = (bf16[256,512]{1,0:T(8,128)(2,1)S(1)}, bf16[256,512]{1,0:T(8,128)(2,1)S(1)}, u32[]{:S(2)}, u32[]{:S(2)}) collective-permute-start(bf16[256,512]{1,0:T(8,128)(2,1)S(1)} %get-tuple-element.51), channel_id=1, source_target_pairs={{0,96},{16,112},{32,0},{48,16},{64,32},{80,48},{96,64},{112,80},{1... | collective-permute-start | bytes 786440 | tf_op jit(solution)/shard_map/down2/ppermute | solution.py:53
  108.7 3.8 %collective-permute-done.11 = bf16[256,512]{1,0:T(8,128)(2,1)S(1)} collective-permute-done((bf16[256,512]{1,0:T(8,128)(2,1)S(1)}, bf16[256,512]{1,0:T(8,128)(2,1)S(1)}, u32[]{:S(2)}, u32[]{:S(2)}) %collective-permute-start.11) | collective-permute-done | bytes 262176 | tf_op jit(solution)/shard_map/up1/ppermute | solution.py:48
  112.6 2.7 %collective-permute-start.16 = (bf16[256,512]{1,0:T(8,128)(2,1)S(1)}, bf16[256,512]{1,0:T(8,128)(2,1)S(1)}, u32[]{:S(2)}, u32[]{:S(2)}) collective-permute-start(bf16[256,512]{1,0:T(8,128)(2,1)S(1)} %collective-permute-done.14), channel_id=1, source_target_pairs={{0,96},{16,112},{32,0},{48,16},{64,32},{80,48},{96,64},{112,80},{1... | collective-permute-start | bytes 786440 | tf_op jit(solution)/shard_map/down3/ppermute | solution.py:53
  115.2 2.9 %collective-permute-done.12 = bf16[256,512]{1,0:T(8,128)(2,1)S(1)} collective-permute-done((bf16[256,512]{1,0:T(8,128)(2,1)S(1)}, bf16[256,512]{1,0:T(8,128)(2,1)S(1)}, u32[]{:S(2)}, u32[]{:S(2)}) %collective-permute-start.12) | collective-permute-done | bytes 262176 | tf_op jit(solution)/shard_map/up2/ppermute | solution.py:48
  118.2 0.8 collective-permute-start.17
  118.9 0.5 collective-permute-start.19
  119.4 4.3 %collective-permute-done.15 = bf16[256,512]{1,0:T(8,128)(2,1)S(1)} collective-permute-done((bf16[256,512]{1,0:T(8,128)(2,1)S(1)}, bf16[256,512]{1,0:T(8,128)(2,1)S(1)}, u32[]{:S(2)}, u32[]{:S(2)}) %collective-permute-start.15) | collective-permute-done | bytes 262176 | tf_op jit(solution)/shard_map/up3/ppermute | solution.py:48
  123.8 0.6 collective-permute-start.20
  124.4 0.5 broadcast_in_dim.23
  124.9 0.1 constant_dynamic-update-slice_fusion.6
  125.1 0.4 collective-permute-done.20
  125.7 0.5 collective-permute-start.21
  126.2 0.2 collective-permute-start.22
  126.5 0.8 collective-permute-done.21
  127.3 0.5 collective-permute-done.22
  127.8 2.0 %copy-done.4 = bf16[512,4096]{1,0:T(8,128)(2,1)} copy-done((bf16[512,4096]{1,0:T(8,128)(2,1)}, bf16[512,4096]{1,0:T(8,128)(2,1)S(1)}, u32[]{:S(2)}) %copy-start.4) | copy-done | bytes 4194328
  (43 shorter events, 0.7 us)
Async XLA Ops:
  0.6 5.5 %copy-start.3 = (s32[16,1]{0,1:T(1,128)S(1)}, s32[16,1]{0,1:T(1,128)}, u32[]{:S(2)}) copy-start(s32[16,1]{0,1:T(1,128)} %param.6) | copy-start | bytes 196
  2.5 3.7 %collective-permute-start = (bf16[512,512]{1,0:T(8,128)(2,1)}, bf16[512,512]{1,0:T(8,128)(2,1)}, u32[]{:S(2)}, u32[]{:S(2)}) collective-permute-start(bf16[512,512]{1,0:T(8,128)(2,1)} %dynamic-slice_bitcast_fusion), channel_id=1, source_target_pairs={{0,16},{16,0},{32,48},{48,32},{64,80},{80,64},{96,112},{112,96},{1... | collective-permute-start | bytes 1572872 | tf_op jit(solution)/shard_map/swap/ppermute | solution.py:43
  5.4 6.2 %collective-permute-start.4 = (bf16[512,512]{1,0:T(8,128)(2,1)S(1)}, bf16[512,512]{1,0:T(8,128)(2,1)S(1)}, u32[]{:S(2)}, u32[]{:S(2)}) collective-permute-start(bf16[512,512]{1,0:T(8,128)(2,1)S(1)} %get-tuple-element.46), channel_id=1, source_target_pairs={{0,16},{16,0},{32,48},{48,32},{64,80},{80,64},{96,112},{112,96},{1... | collective-permute-start | bytes 1572872 | tf_op jit(solution)/shard_map/swap/ppermute | solution.py:43
  5.5 6.1 %collective-permute-start.2 = (bf16[512,512]{1,0:T(8,128)(2,1)S(1)}, bf16[512,512]{1,0:T(8,128)(2,1)S(1)}, u32[]{:S(2)}, u32[]{:S(2)}) collective-permute-start(bf16[512,512]{1,0:T(8,128)(2,1)S(1)} %get-tuple-element.47), channel_id=1, source_target_pairs={{0,16},{16,0},{32,48},{48,32},{64,80},{80,64},{96,112},{112,96},{1... | collective-permute-start | bytes 1572872 | tf_op jit(solution)/shard_map/swap/ppermute | solution.py:43
  6.0 5.6 %collective-permute-start.1 = (bf16[512,512]{1,0:T(8,128)(2,1)S(1)}, bf16[512,512]{1,0:T(8,128)(2,1)S(1)}, u32[]{:S(2)}, u32[]{:S(2)}) collective-permute-start(bf16[512,512]{1,0:T(8,128)(2,1)S(1)} %get-tuple-element.48), channel_id=1, source_target_pairs={{0,16},{16,0},{32,48},{48,32},{64,80},{80,64},{96,112},{112,96},{1... | collective-permute-start | bytes 1572872 | tf_op jit(solution)/shard_map/swap/ppermute | solution.py:43
  7.6 10.2 %collective-permute-start.5 = (bf16[256,512]{1,0:T(8,128)(2,1)S(1)}, bf16[256,512]{1,0:T(8,128)(2,1)S(1)}, u32[]{:S(2)}, u32[]{:S(2)}) collective-permute-start(bf16[256,512]{1,0:T(8,128)(2,1)S(1)} %get-tuple-element.54), channel_id=1, source_target_pairs={{0,32},{16,48},{32,64},{48,80},{64,96},{80,112},{96,0},{112,16},{1... | collective-permute-start | bytes 786440 | tf_op jit(solution)/shard_map/up1/ppermute | solution.py:48
  9.4 8.6 %collective-permute-start.8 = (bf16[256,512]{1,0:T(8,128)(2,1)S(1)}, bf16[256,512]{1,0:T(8,128)(2,1)S(1)}, u32[]{:S(2)}, u32[]{:S(2)}) collective-permute-start(bf16[256,512]{1,0:T(8,128)(2,1)S(1)} %get-tuple-element.53), channel_id=1, source_target_pairs={{0,96},{16,112},{32,0},{48,16},{64,32},{80,48},{96,64},{112,80},{1... | collective-permute-start | bytes 786440 | tf_op jit(solution)/shard_map/down1/ppermute | solution.py:53
  13.4 9.2 %collective-permute-start.3 = (bf16[256,512]{1,0:T(8,128)(2,1)S(1)}, bf16[256,512]{1,0:T(8,128)(2,1)S(1)}, u32[]{:S(2)}, u32[]{:S(2)}) collective-permute-start(bf16[256,512]{1,0:T(8,128)(2,1)S(1)} %slice.48), channel_id=1, source_target_pairs={{0,96},{16,112},{32,0},{48,16},{64,32},{80,48},{96,64},{112,80},{1... | collective-permute-start | bytes 786440 | tf_op jit(solution)/shard_map/down2/ppermute | solution.py:53
  14.9 7.8 %collective-permute-start.7 = (bf16[256,512]{1,0:T(8,128)(2,1)S(1)}, bf16[256,512]{1,0:T(8,128)(2,1)S(1)}, u32[]{:S(2)}, u32[]{:S(2)}) collective-permute-start(bf16[256,512]{1,0:T(8,128)(2,1)S(1)} %slice.50), channel_id=1, source_target_pairs={{0,32},{16,48},{32,64},{48,80},{64,96},{80,112},{96,0},{112,16},{1... | collective-permute-start | bytes 786440 | tf_op jit(solution)/shard_map/up2/ppermute | solution.py:48
  18.0 43.2 %copy-start = (bf16[1,1,2,2,512,512]{5,4,3,2,1,0:T(8,128)(2,1)S(1)}, bf16[1,1,2,2,512,512]{5,4,3,2,1,0:T(8,128)(2,1)}, u32[]{:S(2)}) copy-start(bf16[1,1,2,2,512,512]{5,4,3,2,1,0:T(8,128)(2,1)} %param.7) | copy-start | bytes 6291460
  18.0 43.2 %copy-start.1 = (f32[1,1,2,512,512]{4,3,2,1,0:T(8,128)S(1)}, f32[1,1,2,512,512]{4,3,2,1,0:T(8,128)}, u32[]{:S(2)}) copy-start(f32[1,1,2,512,512]{4,3,2,1,0:T(8,128)} %param.9) | copy-start | bytes 6291460
  18.0 43.1 %copy-start.2 = (bf16[1,1,2,512,512]{4,3,2,1,0:T(8,128)(2,1)S(1)}, bf16[1,1,2,512,512]{4,3,2,1,0:T(8,128)(2,1)}, u32[]{:S(2)}) copy-start(bf16[1,1,2,512,512]{4,3,2,1,0:T(8,128)(2,1)} %param.8) | copy-start | bytes 3145732
  18.0 10.3 %collective-permute-start.6 = (bf16[256,512]{1,0:T(8,128)(2,1)S(1)}, bf16[256,512]{1,0:T(8,128)(2,1)S(1)}, u32[]{:S(2)}, u32[]{:S(2)}) collective-permute-start(bf16[256,512]{1,0:T(8,128)(2,1)S(1)} %add_convert_fusion.4), channel_id=1, source_target_pairs={{0,32},{16,48},{32,64},{48,80},{64,96},{80,112},{96,0},{112,16},{1... | collective-permute-start | bytes 786440 | tf_op jit(solution)/shard_map/up3/ppermute | solution.py:48
  18.2 10.2 %collective-permute-start.9 = (bf16[256,512]{1,0:T(8,128)(2,1)S(1)}, bf16[256,512]{1,0:T(8,128)(2,1)S(1)}, u32[]{:S(2)}, u32[]{:S(2)}) collective-permute-start(bf16[256,512]{1,0:T(8,128)(2,1)S(1)} %add_convert_fusion.3), channel_id=1, source_target_pairs={{0,96},{16,112},{32,0},{48,16},{64,32},{80,48},{96,64},{112,80},{1... | collective-permute-start | bytes 786440 | tf_op jit(solution)/shard_map/down3/ppermute | solution.py:53
  93.4 12.6 %collective-permute-start.10 = (bf16[512,512]{1,0:T(8,128)(2,1)S(1)}, bf16[512,512]{1,0:T(8,128)(2,1)S(1)}, u32[]{:S(2)}, u32[]{:S(2)}) collective-permute-start(bf16[512,512]{1,0:T(8,128)(2,1)S(1)} %bitcast.23), channel_id=1, source_target_pairs={{0,16},{16,0},{32,48},{48,32},{64,80},{80,64},{96,112},{112,96},{1... | collective-permute-start | bytes 1572872 | tf_op jit(solution)/shard_map/swap/ppermute | solution.py:43
  99.9 12.6 %collective-permute-start.11 = (bf16[256,512]{1,0:T(8,128)(2,1)S(1)}, bf16[256,512]{1,0:T(8,128)(2,1)S(1)}, u32[]{:S(2)}, u32[]{:S(2)}) collective-permute-start(bf16[256,512]{1,0:T(8,128)(2,1)S(1)} %bitcast.30), channel_id=1, source_target_pairs={{0,32},{16,48},{32,64},{48,80},{64,96},{80,112},{96,0},{112,16},{1... | collective-permute-start | bytes 786440 | tf_op jit(solution)/shard_map/up1/ppermute | solution.py:48
  101.9 10.6 %collective-permute-start.14 = (bf16[256,512]{1,0:T(8,128)(2,1)S(1)}, bf16[256,512]{1,0:T(8,128)(2,1)S(1)}, u32[]{:S(2)}, u32[]{:S(2)}) collective-permute-start(bf16[256,512]{1,0:T(8,128)(2,1)S(1)} %bitcast.29), channel_id=1, source_target_pairs={{0,96},{16,112},{32,0},{48,16},{64,32},{80,48},{96,64},{112,80},{1... | collective-permute-start | bytes 786440 | tf_op jit(solution)/shard_map/down1/ppermute | solution.py:53
  106.0 12.2 %collective-permute-start.12 = (bf16[256,512]{1,0:T(8,128)(2,1)S(1)}, bf16[256,512]{1,0:T(8,128)(2,1)S(1)}, u32[]{:S(2)}, u32[]{:S(2)}) collective-permute-start(bf16[256,512]{1,0:T(8,128)(2,1)S(1)} %get-tuple-element.52), channel_id=1, source_target_pairs={{0,32},{16,48},{32,64},{48,80},{64,96},{80,112},{96,0},{112,16},{1... | collective-permute-start | bytes 786440 | tf_op jit(solution)/shard_map/up2/ppermute | solution.py:48
  106.1 12.1 %collective-permute-start.13 = (bf16[256,512]{1,0:T(8,128)(2,1)S(1)}, bf16[256,512]{1,0:T(8,128)(2,1)S(1)}, u32[]{:S(2)}, u32[]{:S(2)}) collective-permute-start(bf16[256,512]{1,0:T(8,128)(2,1)S(1)} %get-tuple-element.51), channel_id=1, source_target_pairs={{0,96},{16,112},{32,0},{48,16},{64,32},{80,48},{96,64},{112,80},{1... | collective-permute-start | bytes 786440 | tf_op jit(solution)/shard_map/down2/ppermute | solution.py:53
  112.5 11.2 %collective-permute-start.15 = (bf16[256,512]{1,0:T(8,128)(2,1)S(1)}, bf16[256,512]{1,0:T(8,128)(2,1)S(1)}, u32[]{:S(2)}, u32[]{:S(2)}) collective-permute-start(bf16[256,512]{1,0:T(8,128)(2,1)S(1)} %collective-permute-done.11), channel_id=1, source_target_pairs={{0,32},{16,48},{32,64},{48,80},{64,96},{80,112},{96,0},{112,16},{1... | collective-permute-start | bytes 786440 | tf_op jit(solution)/shard_map/up3/ppermute | solution.py:48
  112.6 12.5 %collective-permute-start.16 = (bf16[256,512]{1,0:T(8,128)(2,1)S(1)}, bf16[256,512]{1,0:T(8,128)(2,1)S(1)}, u32[]{:S(2)}, u32[]{:S(2)}) collective-permute-start(bf16[256,512]{1,0:T(8,128)(2,1)S(1)} %collective-permute-done.14), channel_id=1, source_target_pairs={{0,96},{16,112},{32,0},{48,16},{64,32},{80,48},{96,64},{112,80},{1... | collective-permute-start | bytes 786440 | tf_op jit(solution)/shard_map/down3/ppermute | solution.py:53
  118.2 6.9 %collective-permute-start.17 = (bf16[256,512]{1,0:T(8,128)(2,1)S(1)}, bf16[256,512]{1,0:T(8,128)(2,1)S(1)}, u32[]{:S(2)}, u32[]{:S(2)}) collective-permute-start(bf16[256,512]{1,0:T(8,128)(2,1)S(1)} %collective-permute-done.11), channel_id=1, source_target_pairs={{0,16},{16,0},{32,48},{48,32},{64,80},{80,64},{96,112},{112,96},{1... | collective-permute-start | bytes 786440 | tf_op jit(solution)/shard_map/swap/ppermute | solution.py:43
  118.9 6.2 %collective-permute-start.18 = (bf16[256,512]{1,0:T(8,128)(2,1)S(1)}, bf16[256,512]{1,0:T(8,128)(2,1)S(1)}, u32[]{:S(2)}, u32[]{:S(2)}) collective-permute-start(bf16[256,512]{1,0:T(8,128)(2,1)S(1)} %collective-permute-done.12), channel_id=1, source_target_pairs={{0,16},{16,0},{32,48},{48,32},{64,80},{80,64},{96,112},{112,96},{1... | collective-permute-start | bytes 786440 | tf_op jit(solution)/shard_map/swap/ppermute | solution.py:43
  118.9 6.2 %collective-permute-start.19 = (bf16[256,512]{1,0:T(8,128)(2,1)S(1)}, bf16[256,512]{1,0:T(8,128)(2,1)S(1)}, u32[]{:S(2)}, u32[]{:S(2)}) collective-permute-start(bf16[256,512]{1,0:T(8,128)(2,1)S(1)} %collective-permute-done.13), channel_id=1, source_target_pairs={{0,16},{16,0},{32,48},{48,32},{64,80},{80,64},{96,112},{112,96},{1... | collective-permute-start | bytes 786440 | tf_op jit(solution)/shard_map/swap/ppermute | solution.py:43
  123.8 1.7 %collective-permute-start.20 = (bf16[256,512]{1,0:T(8,128)(2,1)S(1)}, bf16[256,512]{1,0:T(8,128)(2,1)S(1)}, u32[]{:S(2)}, u32[]{:S(2)}) collective-permute-start(bf16[256,512]{1,0:T(8,128)(2,1)S(1)} %collective-permute-done.14), channel_id=1, source_target_pairs={{0,16},{16,0},{32,48},{48,32},{64,80},{80,64},{96,112},{112,96},{1... | collective-permute-start | bytes 786440 | tf_op jit(solution)/shard_map/swap/ppermute | solution.py:43
  125.7 1.6 %collective-permute-start.21 = (bf16[256,512]{1,0:T(8,128)(2,1)S(1)}, bf16[256,512]{1,0:T(8,128)(2,1)S(1)}, u32[]{:S(2)}, u32[]{:S(2)}) collective-permute-start(bf16[256,512]{1,0:T(8,128)(2,1)S(1)} %collective-permute-done.15), channel_id=1, source_target_pairs={{0,16},{16,0},{32,48},{48,32},{64,80},{80,64},{96,112},{112,96},{1... | collective-permute-start | bytes 786440 | tf_op jit(solution)/shard_map/swap/ppermute | solution.py:43
  126.2 1.6 %collective-permute-start.22 = (bf16[256,512]{1,0:T(8,128)(2,1)S(1)}, bf16[256,512]{1,0:T(8,128)(2,1)S(1)}, u32[]{:S(2)}, u32[]{:S(2)}) collective-permute-start(bf16[256,512]{1,0:T(8,128)(2,1)S(1)} %collective-permute-done.16), channel_id=1, source_target_pairs={{0,16},{16,0},{32,48},{48,32},{64,80},{80,64},{96,112},{112,96},{1... | collective-permute-start | bytes 786440 | tf_op jit(solution)/shard_map/swap/ppermute | solution.py:43
  127.8 2.0 %copy-start.4 = (bf16[512,4096]{1,0:T(8,128)(2,1)}, bf16[512,4096]{1,0:T(8,128)(2,1)S(1)}, u32[]{:S(2)}) copy-start(bf16[512,4096]{1,0:T(8,128)(2,1)S(1)} %constant_dynamic-update-slice_fusion.8) | copy-start | bytes 12582916

commit v3 on v2

--- a/solution.py
+++ b/solution.py
@@ -9,21 +9,12 @@
 SLOTS = 2
 PEERS = 16
 PIECE = SIDE // PEERS
-HALF = SIDE // 2
 VMEM_LIMIT = 24 * 1024 * 1024
 
 
-def ring(step):
-    return [(i, ((i // 2 + step) % 4) * 2 + i % 2) for i in range(8)]
-
-
-UP = ring(1)
-DOWN = ring(3)
+NEXT = [(i, (i + 2) % 8) for i in range(0, 8, 2)]
 CORES = [(i, i ^ 1) for i in range(8)]
-
-
-def add(a, b):
-    return (a.astype(jnp.float32) + b.astype(jnp.float32)).astype(jnp.bfloat16)
+PLANES = [[r * PEERS + f for r in range(c, 8, 2) for f in range(PEERS)] for c in range(2)]
 
 
 def vmem_call(kernel, name, out_shape, *operands):
@@ -43,62 +34,50 @@
         return lax.ppermute(x, "replica", CORES)
 
 
-def up(x, name):
-    with jax.named_scope(name):
-        return lax.ppermute(x, "replica", UP)
-
-
-def down(x, name):
-    with jax.named_scope(name):
-        return lax.ppermute(x, "replica", DOWN)
-
-
-def home_kernel(a_ref, t1_ref, t2_ref, l1_ref, l2_ref, o_ref):
-    for n, (x_ref, y_ref) in enumerate(((t1_ref, t2_ref), (l1_ref, l2_ref))):
-        rows = pl.ds(n * HALF, HALF)
-        total = a_ref[rows] + x_ref[...].astype(jnp.float32) + y_ref[...].astype(jnp.float32)
-        o_ref[rows] = total.astype(jnp.bfloat16)
-
-
-def sum_replicas(grads, z, core, extra):
-    def part(x, d, which):
-        col = (lax.rem(z + d, 4) * 2 + which) * SIDE
-        return lax.dynamic_slice(x, (0, col), (SIDE, SIDE))
-
-    def halves(x):
-        x = x.astype(jnp.bfloat16)
-        return x[:HALF], x[HALF:]
-
-    def both(x, d, got):
-        return part(x, d, core).astype(jnp.float32) + got.astype(jnp.float32)
-
-    give2 = part(grads, 2, 1 - core)
-    later, give2 = lax.optimization_barrier((grads, give2))
-    got2 = swap(give2)
-    got1, got3, got0 = (swap(part(later, d, 1 - core)) for d in (1, 3, 0))
-    s2 = both(later, 2, got2).astype(jnp.bfloat16)
-    later, s2, extra = lax.optimization_barrier((later, s2, extra))
-    top2, low2 = halves(s2)
-    up1, down1 = up(top2, "up1"), down(low2, "down1")
-    top1, low1 = halves(both(later, 1, got1))
-    top3, low3 = halves(both(later, 3, got3))
-    up2, down2 = up(low1, "up2"), down(top3, "down2")
-    up3, down3 = up(add(top1, up1), "up3"), down(add(low3, down1), "down3")
-    shape = jax.ShapeDtypeStruct((SIDE, SIDE), jnp.bfloat16)
-    home = vmem_call(home_kernel, "home", shape, both(later, 0, got0), down2, up3, up2, down3)
-    return home, extra
-
-
-def pick_kernel(index_ref, x_ref, o_ref):
+def exchange(x):
+    return lax.all_to_all(
+        x, ("replica", "fsdp"), 0, 0, tiled=True, axis_index_groups=PLANES
+    )
+
+
+def sum_kernel(a_ref, b_ref, after_ref, o_ref):
+    for z in range(4):
+        total = a_ref[z].astype(jnp.float32) + b_ref[z].astype(jnp.float32)
+        o_ref[z] = total.astype(jnp.bfloat16)
+
+
+def core_sums(grads, core):
+    def part(z, which):
+        return lax.dynamic_slice(grads, (0, (2 * z + which) * SIDE), (SIDE, SIDE))
+
+    give = jnp.stack([part(z, 1 - core) for z in range(4)])
+    got = swap(give)
+    x = give[0, :16, :128]
+    for _ in range(2):
+        with jax.named_scope("hop"):
+            x = lax.ppermute(x, "replica", NEXT)
+    own = jnp.stack([part(z, core) for z in range(4)])
+    return vmem_call(sum_kernel, "sum", jax.ShapeDtypeStruct(own.shape, own.dtype), own, got, x)
+
+
+def pick_sum_kernel(index_ref, x_ref, o_ref):
     for t in range(o_ref.shape[0]):
         i = index_ref[t]
-        v = x_ref[jnp.maximum(i, 0)]
-        o_ref[t] = jnp.where(i >= 0, v, jnp.zeros_like(v))
-
-
-def pick(index, x, count):
+        at = jnp.maximum(i, 0)
+        v = sum(x_ref[z * PEERS + at].astype(jnp.float32) for z in range(4))
+        o_ref[t] = jnp.where(i >= 0, v, jnp.zeros_like(v)).astype(jnp.bfloat16)
+
+
+def pick_copies_kernel(index_ref, x_ref, o_ref):
+    for t in range(PEERS):
+        v = x_ref[index_ref[t]]
+        for z in range(4):
+            o_ref[z * PEERS + t] = v
+
+
+def pick(kernel, index, x, count):
     return pl.pallas_call(
-        pick_kernel,
+        kernel,
         out_shape=jax.ShapeDtypeStruct((count,) + x.shape[1:], x.dtype),
         in_specs=[
             pl.BlockSpec(memory_space=pltpu.SMEM),
@@ -184,39 +163,27 @@
     )(g, factors, momentum, accum)
 
 
-def gather_replicas(tile, z, core):
-    up1, down1 = up(tile[:HALF], "up1"), down(tile[HALF:], "down1")
-    tile, own = lax.optimization_barrier((tile, swap(tile)))
-    up2, down2 = up(tile[HALF:], "up2"), down(tile[:HALF], "down2")
-    up3, down3 = up(up1, "up3"), down(down1, "down3")
-    near = lax.optimization_barrier((up1, up2, down2, down1))
-    other = [swap(x) for x in near]
-    up3, down3, *other = lax.optimization_barrier((up3, down3, *other))
-    out = jnp.zeros((SIDE, 8 * SIDE), tile.dtype)
-
-    def put(out, x, row, d, which):
-        return lax.dynamic_update_slice(out, x, (row, (lax.rem(z + d, 4) * 2 + which) * SIDE))
-
-    out = put(put(out, tile, 0, 0, core), own, 0, 0, 1 - core)
-    halves = [*zip(near, other), (up3, swap(up3)), (down3, swap(down3))]
-    for n, (x, y) in enumerate(halves):
-        row, d = n % 2 * HALF, (3, 1, 2)[n // 2]
-        out = put(put(out, x, row, d, core), y, row, d, 1 - core)
+def gather_cores(blocks, core):
+    other = swap(blocks)
+    out = jnp.zeros((SIDE, 8 * SIDE), blocks.dtype)
+    for z in range(4):
+        out = lax.dynamic_update_slice(out, blocks[z], (0, (2 * z + core) * SIDE))
+        out = lax.dynamic_update_slice(out, other[z], (0, (2 * z + 1 - core) * SIDE))
     return out
 
 
 def body(grads, owners, factors, momentum, accum):
-    replica = lax.axis_index("replica")
-    z, core = replica // 2, lax.rem(replica, 2)
+    core = lax.rem(lax.axis_index("replica"), 2)
     ids = owners[:, 0]
     named = ids[None, :] == jnp.arange(PEERS * SLOTS, dtype=jnp.int32)[:, None]
     block_of = jnp.max(
         jnp.where(named, jnp.arange(PEERS, dtype=jnp.int32)[None, :], -1), axis=1
     )
 
-    home, block_of = sum_replicas(grads[0], z, core, block_of)
-    pieces = lax.all_to_all(home.reshape(PEERS, PIECE, SIDE), "fsdp", 0, 0, tiled=True)
-    routed = pick(block_of, pieces, PEERS * SLOTS)
+    sums = core_sums(grads[0], core)
+    sums, block_of = lax.optimization_barrier((sums, block_of))
+    pieces = exchange(sums.reshape(4 * PEERS, PIECE, SIDE))
+    routed = pick(pick_sum_kernel, block_of, pieces, PEERS * SLOTS)
     slot_grad = lax.all_to_all(
         routed.reshape(PEERS, SLOTS, PIECE, SIDE), "fsdp", 0, 0, tiled=True
     )
@@ -224,9 +191,9 @@
         slot_grad, factors[0, 0], momentum[0, 0], accum[0, 0]
     )
     back = lax.all_to_all(update, "fsdp", 0, 0, tiled=True)
-    back = pick(ids, back.reshape(PEERS * SLOTS, PIECE, SIDE), PEERS)
-    tile = lax.all_to_all(back, "fsdp", 0, 0, tiled=True).reshape(SIDE, SIDE)
-    out = gather_replicas(tile, z, core)
+    back = back.reshape(PEERS * SLOTS, PIECE, SIDE)
+    blocks = exchange(pick(pick_copies_kernel, ids, back, 4 * PEERS))
+    out = gather_cores(blocks.reshape(4, SIDE, SIDE), core)
     return (out, moment_new[None, None], squares_new[None, None])
 
 

time: 130 us -> 120 us (0.923)
  blocking collectives: 59.8 us -> 86.1 us
  waiting for transfers between devices: 23.1 us -> 4.33 us
  starting transfers between devices: 30.9 us -> 15.7 us
  other arithmetic: 3.3 us -> 0.62 us
    all_to_all x2, blocking collectives: 27.6 us -> 57 us  [exchange(): lax.all_to_all(x, ('replica', 'fsdp'), 0, 0, tiled=True, axis_index_group...]
    ppermute x12 -> x2, waiting for transfers between devices: 21.4 us -> 0.01 us  [core_sums(): x = lax.ppermute(x, 'replica', NEXT)]
    ppermute x12 -> x2, starting transfers between devices: 19.8 us -> 1.31 us  [core_sums(): x = lax.ppermute(x, 'replica', NEXT)]
    ppermute x11 -> x2, starting transfers between devices: 11.1 us -> 14.4 us  [swap(): return lax.ppermute(x, 'replica', CORES)]
    convert_element_type x4 -> x0, other arithmetic: 3.21 us -> none  [the longest x1 1.73 us: halves(): x = x.astype(jnp.bfloat16)]
    ppermute x11 -> x2, waiting for transfers between devices: 1.71 us -> 4.33 us  [swap(): return lax.ppermute(x, 'replica', CORES)]
    all_to_all x1, blocking collectives: 16.1 us -> 14.5 us  [body(): back = lax.all_to_all(update, 'fsdp', 0, 0, tiled=True)]
    all_to_all x1, blocking collectives: 16 us -> 14.6 us  [body(): lax.all_to_all(routed.reshape(PEERS, SLOTS, PIECE, SIDE), 'fsdp', 0, 0, t...]
  transfers between devices with their start and end apart: 23 -> 4, of which waited for: 10 -> 2; matrix products, arithmetic and copies ran while one was open for 4% -> 2% of each run, Pallas kernels for 0% -> 0%
where the time goes in v3:
time: 120 us
  blocking collectives  86.1 us (72%)
  starting transfers between devices  15.7 us (13%)
  local copies, waits for them, and re-layouts  6.48 us (5%)
  Pallas kernels  6.02 us (5%)
  waiting for transfers between devices  4.33 us (4%)
    all_to_all x2, blocking collectives, exchange(): lax.all_to_all(x, ('replica', 'fsdp'), 0, 0, tiled=True, axis_index_group...  57 us
    all_to_all x1, blocking collectives, body(): lax.all_to_all(routed.reshape(PEERS, SLOTS, PIECE, SIDE), 'fsdp', 0, 0, t...  14.6 us
    all_to_all x1, blocking collectives, body(): back = lax.all_to_all(update, 'fsdp', 0, 0, tiled=True)  14.5 us
    ppermute x2, starting transfers between devices, swap(): return lax.ppermute(x, 'replica', CORES)  14.4 us
    ppermute x2, waiting for transfers between devices, swap(): return lax.ppermute(x, 'replica', CORES)  4.33 us
    pallas_call x1, Pallas kernels, slot_step(): pl.pallas_call(slot_kernel, out_shape=(jax.ShapeDtypeStruct(slots, jnp.bf...  3.74 us
    dynamic_slice x1, local copies, waits for them, and re-layouts, part(): return lax.dynamic_slice(grads, (0, (2 * z + which) * SIDE), (SIDE, SIDE))  2.47 us
  transfers between devices with their start and end apart: 4, of which 2 were waited for; matrix products, arithmetic and copies ran while one was open for 2% of the time, Pallas kernels for 0%

profile of v3, /device:TPU:1, one launch (start us, length us, event | category | flops | bytes accessed | tf_op | source)
XLA Modules:
  0.0 120.0 jit_solution(7970377235863516585)
XLA Ops:
  0.7 2.5 %constant_dynamic-slice_fusion.4 = (bf16[1,512,512]{2,1,0:T(8,128)(2,1)S(1)}, bf16[1,512,512]{2,1,0:T(8,128)(2,1)S(1)}, bf16[1,512,512]{2,1,0:T(8,128)(2,1)S(1)}...) fusion(bf16[1,512,4096]{2,1,0:T(8,128)(2,1)} %param.5, ...), kind=kLoop, calls=%fused_computation.20 | loop fusion | bytes 8388640 | tf_op jit(solution)/shard_map/dynamic_slice | solution.py:51
  3.1 0.3 pad_maximum_fusion.1
  3.4 1.5 %collective-permute-start = (bf16[4,512,512]{2,1,0:T(8,128)(2,1)S(1)}, bf16[4,512,512]{2,1,0:T(8,128)(2,1)S(1)}, u32[]{:S(2)}, u32[]{:S(2)}) collective-permute-start(bf16[4,512,512]{2,1,0:T(8,128)(2,1)S(1)} %pad_maximum_fusion.1), channel_id=1, source_target_pairs={{0,16},{16,0},{32,48},{48,32},{64,80},{80,64},{96,112},{112,96},{1... | collective-permute-start | bytes 6291464 | tf_op jit(solution)/shard_map/swap/ppermute | solution.py:34
  4.9 0.7 fusion.4
  5.6 0.6 collective-permute-start.1
  6.2 0.0 copy-start.3
  6.3 0.3 pad_maximum_fusion.a_ref
  6.5 0.0 collective-permute-done.1
  6.5 0.7 collective-permute-start.2
  7.2 0.0 copy-done.3
  7.2 0.1 select_reduce_fusion.index_ref
  7.3 0.0 collective-permute-done.2.after_ref
  7.3 1.4 %collective-permute-done.b_ref = bf16[4,512,512]{2,1,0:T(8,128)(2,1)S(1)} collective-permute-done((bf16[4,512,512]{2,1,0:T(8,128)(2,1)S(1)}, bf16[4,512,512]{2,1,0:T(8,128)(2,1)S(1)}, u32[]{:S(2)}, u32[]{:S(2)}) %collective-permute-start) | collective-permute-done | bytes 2097184 | tf_op jit(solution)/shard_map/swap/ppermute | solution.py:34
  8.7 0.5 sum.1
  9.2 33.8 %all_to_all.20.x_ref = bf16[64,32,512]{2,1,0:T(8,128)(2,1)S(1)} all-to-all(bf16[64,32,512]{2,1,0:T(8,128)(2,1)S(1)} %bitcast.32), channel_id=1, replica_groups={{0,1,2,3,4,5,6,7,8,9,10,11,12,13,14,15,32,33,34,35,36,37,38,39,40,41,42..., dimensions={0} | all-to-all | bytes 4194304 | tf_op jit(solution)/shard_map/all_to_all | solution.py:38
  43.0 0.0 copy-start
  43.0 0.0 copy-start.1
  43.0 0.0 copy-start.2
  43.0 1.1 pick.2
  44.1 14.6 %all_to_all.21.g_ref = bf16[16,2,32,512]{3,2,1,0:T(8,128)(2,1)S(1)} all-to-all(bf16[16,2,32,512]{3,2,1,0:T(8,128)(2,1)S(1)} %bitcast.33), channel_id=1, replica_groups=mesh['replica'=8,'fsdp'=16] {'fsdp'}, dimensions={0} | all-to-all | bytes 2097152 | tf_op jit(solution)/shard_map/all_to_all | solution.py:187
  58.7 0.0 copy-done
  58.7 0.0 copy-done.1
  58.7 0.0 copy-done.2
  58.7 3.7 %slot_step.1 = (bf16[2,512,512]{2,1,0:T(8,128)(2,1)}, f32[2,512,512]{2,1,0:T(8,128)}, bf16[16,2,32,512]{3,2,1,0:T(8,128)(2,1)S(1)}) custom-call(bf16[16,2,32,512]{3,2,1,0:T(8,128)(2,1)S(1)} %all_to_all.21.g_ref, bf16[2,2,512,512]{3,2,1,0:T(8,128)(2,1)S(1)} %bitcast.35, bf16[2,512,512]{2,1,0:T(8,128)(2,1)S(1)} %bitcast.37, f32[2,512,512]{2,1,0:T(8,128)S(1)} %bitcast.36), custom_call_target="tpu_custom_call" | custom-call | tf_op jit(solution)/shard_map/slot_step/pallas_call | solution.py:142
  62.5 14.5 %all_to_all.22 = bf16[16,2,32,512]{3,2,1,0:T(8,128)(2,1)S(1)} all-to-all(bf16[16,2,32,512]{3,2,1,0:T(8,128)(2,1)S(1)} %get-tuple-element.10), channel_id=1, replica_groups=mesh['replica'=8,'fsdp'=16] {'fsdp'}, dimensions={0} | all-to-all | bytes 2097152 | tf_op jit(solution)/shard_map/all_to_all | solution.py:193
  76.9 0.7 pick.3
  77.6 23.2 %all_to_all.23 = bf16[64,32,512]{2,1,0:T(8,128)(2,1)S(1)} all-to-all(bf16[64,32,512]{2,1,0:T(8,128)(2,1)S(1)} %pick.3), channel_id=1, replica_groups={{0,1,2,3,4,5,6,7,8,9,10,11,12,13,14,15,32,33,34,35,36,37,38,39,40,41,42..., dimensions={0} | all-to-all | bytes 4194304 | tf_op jit(solution)/shard_map/all_to_all | solution.py:38
  100.8 12.9 %collective-permute-start.3 = (bf16[4,512,512]{2,1,0:T(8,128)(2,1)S(1)}, bf16[4,512,512]{2,1,0:T(8,128)(2,1)S(1)}, u32[]{:S(2)}, u32[]{:S(2)}) collective-permute-start(bf16[4,512,512]{2,1,0:T(8,128)(2,1)S(1)} %bitcast.40), channel_id=1, source_target_pairs={{0,16},{16,0},{32,48},{48,32},{64,80},{80,64},{96,112},{112,96},{1... | collective-permute-start | bytes 6291464 | tf_op jit(solution)/shard_map/swap/ppermute | solution.py:34
  113.7 0.2 fusion.5
  113.9 0.5 broadcast_in_dim.23
  114.5 0.1 constant_dynamic-update-slice_fusion.3
  114.5 3.0 %collective-permute-done.3 = bf16[4,512,512]{2,1,0:T(8,128)(2,1)S(1)} collective-permute-done((bf16[4,512,512]{2,1,0:T(8,128)(2,1)S(1)}, bf16[4,512,512]{2,1,0:T(8,128)(2,1)S(1)}, u32[]{:S(2)}, u32[]{:S(2)}) %collective-permute-start.3) | collective-permute-done | bytes 2097184 | tf_op jit(solution)/shard_map/swap/ppermute | solution.py:34
  117.5 0.1 fusion.3
  117.6 0.1 constant_dynamic-update-slice_fusion.2
  117.6 0.1 fusion.2
  117.7 0.1 constant_dynamic-update-slice_fusion.1
  117.8 0.1 fusion.1
  117.9 0.1 constant_dynamic-update-slice_fusion
  117.9 0.1 fusion
  118.0 0.0 copy-start.4
  118.0 2.0 %copy-done.4 = bf16[512,4096]{1,0:T(8,128)(2,1)} copy-done((bf16[512,4096]{1,0:T(8,128)(2,1)}, bf16[512,4096]{1,0:T(8,128)(2,1)S(1)}, u32[]{:S(2)}) %copy-start.4) | copy-done | bytes 4194328
Async XLA Ops:
  3.4 5.3 %collective-permute-start = (bf16[4,512,512]{2,1,0:T(8,128)(2,1)S(1)}, bf16[4,512,512]{2,1,0:T(8,128)(2,1)S(1)}, u32[]{:S(2)}, u32[]{:S(2)}) collective-permute-start(bf16[4,512,512]{2,1,0:T(8,128)(2,1)S(1)} %pad_maximum_fusion.1), channel_id=1, source_target_pairs={{0,16},{16,0},{32,48},{48,32},{64,80},{80,64},{96,112},{112,96},{1... | collective-permute-start | bytes 6291464 | tf_op jit(solution)/shard_map/swap/ppermute | solution.py:34
  5.6 0.9 collective-permute-start.1
  6.2 1.0 copy-start.3
  6.5 0.8 collective-permute-start.2
  43.0 15.7 %copy-start = (bf16[1,1,2,2,512,512]{5,4,3,2,1,0:T(8,128)(2,1)S(1)}, bf16[1,1,2,2,512,512]{5,4,3,2,1,0:T(8,128)(2,1)}, u32[]{:S(2)}) copy-start(bf16[1,1,2,2,512,512]{5,4,3,2,1,0:T(8,128)(2,1)} %param.7) | copy-start | bytes 6291460
  43.0 15.7 %copy-start.1 = (f32[1,1,2,512,512]{4,3,2,1,0:T(8,128)S(1)}, f32[1,1,2,512,512]{4,3,2,1,0:T(8,128)}, u32[]{:S(2)}) copy-start(f32[1,1,2,512,512]{4,3,2,1,0:T(8,128)} %param.9) | copy-start | bytes 6291460
  43.0 15.7 %copy-start.2 = (bf16[1,1,2,512,512]{4,3,2,1,0:T(8,128)(2,1)S(1)}, bf16[1,1,2,512,512]{4,3,2,1,0:T(8,128)(2,1)}, u32[]{:S(2)}) copy-start(bf16[1,1,2,512,512]{4,3,2,1,0:T(8,128)(2,1)} %param.8) | copy-start | bytes 3145732
  100.8 16.6 %collective-permute-start.3 = (bf16[4,512,512]{2,1,0:T(8,128)(2,1)S(1)}, bf16[4,512,512]{2,1,0:T(8,128)(2,1)S(1)}, u32[]{:S(2)}, u32[]{:S(2)}) collective-permute-start(bf16[4,512,512]{2,1,0:T(8,128)(2,1)S(1)} %bitcast.40), channel_id=1, source_target_pairs={{0,16},{16,0},{32,48},{48,32},{64,80},{80,64},{96,112},{112,96},{1... | collective-permute-start | bytes 6291464 | tf_op jit(solution)/shard_map/swap/ppermute | solution.py:34
  118.0 2.0 %copy-start.4 = (bf16[512,4096]{1,0:T(8,128)(2,1)}, bf16[512,4096]{1,0:T(8,128)(2,1)S(1)}, u32[]{:S(2)}) copy-start(bf16[512,4096]{1,0:T(8,128)(2,1)S(1)} %fusion) | copy-start | bytes 12582916

commit v4 on v3

--- a/solution.py
+++ b/solution.py
@@ -12,7 +12,7 @@
 VMEM_LIMIT = 24 * 1024 * 1024
 
 
-NEXT = [(i, (i + 2) % 8) for i in range(0, 8, 2)]
+NEXT = [(i, i ^ 2) for i in range(0, 8, 2)]
 CORES = [(i, i ^ 1) for i in range(8)]
 PLANES = [[r * PEERS + f for r in range(c, 8, 2) for f in range(PEERS)] for c in range(2)]
 
@@ -40,32 +40,40 @@
     )
 
 
-def sum_kernel(a_ref, b_ref, after_ref, o_ref):
-    for z in range(4):
-        total = a_ref[z].astype(jnp.float32) + b_ref[z].astype(jnp.float32)
+def sum_kernel(own_ref, a_ref, b_ref, after_ref, o_ref):
+    for z, other in enumerate((a_ref[0], a_ref[1], b_ref[0], b_ref[1])):
+        total = own_ref[z].astype(jnp.float32) + other.astype(jnp.float32)
         o_ref[z] = total.astype(jnp.bfloat16)
 
 
 def core_sums(grads, core):
-    def part(z, which):
-        return lax.dynamic_slice(grads, (0, (2 * z + which) * SIDE), (SIDE, SIDE))
-
-    give = jnp.stack([part(z, 1 - core) for z in range(4)])
-    got = swap(give)
-    x = give[0, :16, :128]
+    def part(x, z, which):
+        return lax.dynamic_slice(x, (0, (2 * z + which) * SIDE), (SIDE, SIDE))
+
+    give_a = jnp.stack([part(grads, z, 1 - core) for z in (0, 1)])
+    later, give_a = lax.optimization_barrier((grads, give_a))
+    got_a = swap(give_a)
+    got_b = swap(jnp.stack([part(later, z, 1 - core) for z in (2, 3)]))
+    x = give_a[0, :16, :128]
     for _ in range(2):
         with jax.named_scope("hop"):
             x = lax.ppermute(x, "replica", NEXT)
-    own = jnp.stack([part(z, core) for z in range(4)])
-    return vmem_call(sum_kernel, "sum", jax.ShapeDtypeStruct(own.shape, own.dtype), own, got, x)
+    own = jnp.stack([part(later, z, core) for z in range(4)])
+    return vmem_call(sum_kernel, "sum", jax.ShapeDtypeStruct(own.shape, own.dtype), own, got_a, got_b, x)
 
 
 def pick_sum_kernel(index_ref, x_ref, o_ref):
     for t in range(o_ref.shape[0]):
         i = index_ref[t]
-        at = jnp.maximum(i, 0)
-        v = sum(x_ref[z * PEERS + at].astype(jnp.float32) for z in range(4))
-        o_ref[t] = jnp.where(i >= 0, v, jnp.zeros_like(v)).astype(jnp.bfloat16)
+
+        @pl.when(i >= 0)
+        def _():
+            v = sum(x_ref[z * PEERS + i].astype(jnp.float32) for z in range(4))
+            o_ref[t] = v.astype(jnp.bfloat16)
+
+        @pl.when(i < 0)
+        def _():
+            o_ref[t] = jnp.zeros_like(o_ref[t])
 
 
 def pick_copies_kernel(index_ref, x_ref, o_ref):
@@ -163,13 +171,38 @@
     )(g, factors, momentum, accum)
 
 
+def store_kernel(cols_ref, x_ref, *refs):
+    o_ref, sems = refs[-2:]
+    copies = []
+    for n in range(x_ref.shape[0]):
+        to = o_ref.at[:, pl.ds(pl.multiple_of(cols_ref[n] * SIDE, SIDE), SIDE)]
+        copies.append(pltpu.make_async_copy(x_ref.at[n], to, sems.at[n]))
+    for c in copies:
+        c.start()
+    for c in copies:
+        c.wait()
+
+
+def store(x, cols, *out):
+    hbm = pl.BlockSpec(memory_space=pltpu.HBM)
+    specs = [pl.BlockSpec(memory_space=pltpu.SMEM), pl.BlockSpec(memory_space=pltpu.VMEM)]
+    return pl.pallas_call(
+        store_kernel,
+        out_shape=jax.ShapeDtypeStruct((SIDE, 8 * SIDE), x.dtype),
+        in_specs=specs + [hbm] * len(out),
+        out_specs=hbm,
+        scratch_shapes=[pltpu.SemaphoreType.DMA((x.shape[0],))],
+        input_output_aliases={2: 0} if out else {},
+        compiler_params=pltpu.CompilerParams(vmem_limit_bytes=VMEM_LIMIT),
+        name="store",
+    )(jnp.stack(cols), x, *out)
+
+
 def gather_cores(blocks, core):
-    other = swap(blocks)
-    out = jnp.zeros((SIDE, 8 * SIDE), blocks.dtype)
-    for z in range(4):
-        out = lax.dynamic_update_slice(out, blocks[z], (0, (2 * z + core) * SIDE))
-        out = lax.dynamic_update_slice(out, other[z], (0, (2 * z + 1 - core) * SIDE))
-    return out
+    first, second = swap(blocks[:2]), swap(blocks[2:])
+    out = store(blocks, [2 * z + core for z in range(4)])
+    out = store(first, [2 * z + 1 - core for z in (0, 1)], out)
+    return store(second, [2 * z + 1 - core for z in (2, 3)], out)
 
 
 def body(grads, owners, factors, momentum, accum):

time: 120 us -> 119 us (level)
  Pallas kernels: 6.02 us -> 11 us
  waiting for transfers between devices: 4.33 us -> 0.96 us
  local copies, waits for them, and re-layouts: 6.48 us -> 3.49 us
    pallas_call x0 -> x3, Pallas kernels: none -> 4.95 us  [store(): pl.pallas_call(store_kernel, out_shape=jax.ShapeDtypeStruct((SIDE, 8 * SI...]
    ppermute x2 -> x4, waiting for transfers between devices: 4.33 us -> 0.95 us  [swap(): return lax.ppermute(x, 'replica', CORES)]
    another operation x0 -> x1, local copies, waits for them, and re-layouts: none -> 2.05 us  [core_sums(): got_b = swap(jnp.stack([part(later, z, 1 - core) for z in (2, 3)]))]
    unnamed x10 -> x8, local copies, waits for them, and re-layouts: 2.03 us -> 0.02 us
    ppermute x2 -> x4, starting transfers between devices: 14.4 us -> 15.2 us  [swap(): return lax.ppermute(x, 'replica', CORES)]
  transfers between devices with their start and end apart: 4 -> 6, of which waited for: 2 -> 2; matrix products, arithmetic and copies ran while one was open for 2% -> 2% of each run, Pallas kernels for 0% -> 3%
where the time goes in v4:
time: 119 us
  blocking collectives  85.6 us (72%)
  starting transfers between devices  16.5 us (14%)
  Pallas kernels  11 us (9%)
  local copies, waits for them, and re-layouts  3.49 us (3%)
    all_to_all x2, blocking collectives, exchange(): lax.all_to_all(x, ('replica', 'fsdp'), 0, 0, tiled=True, axis_index_group...  56.3 us
    ppermute x4, starting transfers between devices, swap(): return lax.ppermute(x, 'replica', CORES)  15.2 us
    all_to_all x1, blocking collectives, body(): lax.all_to_all(routed.reshape(PEERS, SLOTS, PIECE, SIDE), 'fsdp', 0, 0, t...  14.8 us
    all_to_all x1, blocking collectives, body(): back = lax.all_to_all(update, 'fsdp', 0, 0, tiled=True)  14.5 us
    pallas_call x3, Pallas kernels, store(): pl.pallas_call(store_kernel, out_shape=jax.ShapeDtypeStruct((SIDE, 8 * SI...  4.95 us
    pallas_call x1, Pallas kernels, slot_step(): pl.pallas_call(slot_kernel, out_shape=(jax.ShapeDtypeStruct(slots, jnp.bf...  3.75 us
  transfers between devices with their start and end apart: 6, of which 2 were waited for; matrix products, arithmetic and copies ran while one was open for 2% of the time, Pallas kernels for 3%

profile of v4, /device:TPU:1, one launch (start us, length us, event | category | flops | bytes accessed | tf_op | source)
XLA Modules:
  0.0 119.1 jit_solution(8661698518715046255)
XLA Ops:
  0.6 1.3 %constant_dynamic-slice_fusion.1 = (bf16[1,512,512]{2,1,0:T(8,128)(2,1)S(1)}, bf16[1,512,512]{2,1,0:T(8,128)(2,1)S(1)}) fusion(bf16[1,512,4096]{2,1,0:T(8,128)(2,1)} %param.5, s32[]{:T(128)S(6)} %select_n.28, s32[]{:T(128)S(6)} %select_n.29), kind=kLoop, calls=%fused_computation.13 | loop fusion | bytes 2097160 | tf_op jit(solution)/shard_map/dynamic_slice | solution.py:51
  1.9 0.1 pad_maximum_fusion.1
  2.0 1.5 %collective-permute-start = (bf16[2,512,512]{2,1,0:T(8,128)(2,1)S(1)}, bf16[2,512,512]{2,1,0:T(8,128)(2,1)S(1)}, u32[]{:S(2)}, u32[]{:S(2)}) collective-permute-start(bf16[2,512,512]{2,1,0:T(8,128)(2,1)S(1)} %pad_maximum_fusion.1), channel_id=1, source_target_pairs={{0,16},{16,0},{32,48},{48,32},{64,80},{80,64},{96,112},{112,96},{1... | collective-permute-start | bytes 3145736 | tf_op jit(solution)/shard_map/swap/ppermute | solution.py:34
  3.5 2.1 %dynamic-slice_bitcast_fusion.1 = (bf16[1,512,512]{2,1,0:T(8,128)(2,1)S(1)}, bf16[1,512,512]{2,1,0:T(8,128)(2,1)S(1)}, bf16[1,512,512]{2,1,0:T(8,128)(2,1)S(1)},...) fusion(bf16[512,4096]{1,0:T(8,128)(2,1)} %bitcast.44, ...), kind=kLoop, calls=%fused_computation.4 | loop fusion | bytes 6291480 | tf_op jit(solution)/shard_map/stack | solution.py:56
  5.6 0.1 pad_maximum_fusion.2
  5.7 0.1 collective-permute-start.1
  5.8 0.6 collective-permute-start.2
  6.5 0.0 copy-start.3
  6.5 0.3 pad_maximum_fusion.own_ref
  6.8 0.0 collective-permute-done.2
  6.8 0.7 collective-permute-start.3
  7.4 0.0 copy-done.3
  7.4 0.1 select_reduce_fusion.index_ref
  7.5 0.0 collective-permute-done.3.after_ref
  7.5 0.0 collective-permute-done.a_ref
  7.6 0.9 collective-permute-done.1.b_ref
  8.4 0.5 sum.1
  8.9 31.9 %all_to_all.20.x_ref = bf16[64,32,512]{2,1,0:T(8,128)(2,1)S(1)} all-to-all(bf16[64,32,512]{2,1,0:T(8,128)(2,1)S(1)} %bitcast.36), channel_id=1, replica_groups={{0,1,2,3,4,5,6,7,8,9,10,11,12,13,14,15,32,33,34,35,36,37,38,39,40,41,42..., dimensions={0} | all-to-all | bytes 4194304 | tf_op jit(solution)/shard_map/all_to_all | solution.py:38
  40.8 0.0 copy-start
  40.8 0.0 copy-start.1
  40.8 0.0 copy-start.2
  40.8 1.2 %pick.2 = bf16[32,32,512]{2,1,0:T(8,128)(2,1)S(1)} custom-call(s32[32]{0:T(128)S(1)} %select_reduce_fusion.index_ref, bf16[64,32,512]{2,1,0:T(8,128)(2,1)S(1)} %all_to_all.20.x_ref), custom_call_target="tpu_custom_call" | custom-call | tf_op jit(solution)/shard_map/pick/pallas_call | solution.py:87
  42.0 14.8 %all_to_all.21.g_ref = bf16[16,2,32,512]{3,2,1,0:T(8,128)(2,1)S(1)} all-to-all(bf16[16,2,32,512]{3,2,1,0:T(8,128)(2,1)S(1)} %bitcast.37), channel_id=1, replica_groups=mesh['replica'=8,'fsdp'=16] {'fsdp'}, dimensions={0} | all-to-all | bytes 2097152 | tf_op jit(solution)/shard_map/all_to_all | solution.py:220
  56.8 0.0 copy-done
  56.8 0.0 copy-done.1
  56.8 0.0 copy-done.2
  56.8 3.7 %slot_step.1 = (bf16[2,512,512]{2,1,0:T(8,128)(2,1)}, f32[2,512,512]{2,1,0:T(8,128)}, bf16[16,2,32,512]{3,2,1,0:T(8,128)(2,1)S(1)}) custom-call(bf16[16,2,32,512]{3,2,1,0:T(8,128)(2,1)S(1)} %all_to_all.21.g_ref, bf16[2,2,512,512]{3,2,1,0:T(8,128)(2,1)S(1)} %bitcast.39, bf16[2,512,512]{2,1,0:T(8,128)(2,1)S(1)} %bitcast.41, f32[2,512,512]{2,1,0:T(8,128)S(1)} %bitcast.40), custom_call_target="tpu_custom_call" | custom-call | tf_op jit(solution)/shard_map/slot_step/pallas_call | solution.py:150
  60.6 14.5 %all_to_all.22 = bf16[16,2,32,512]{3,2,1,0:T(8,128)(2,1)S(1)} all-to-all(bf16[16,2,32,512]{3,2,1,0:T(8,128)(2,1)S(1)} %get-tuple-element.14), channel_id=1, replica_groups=mesh['replica'=8,'fsdp'=16] {'fsdp'}, dimensions={0} | all-to-all | bytes 2097152 | tf_op jit(solution)/shard_map/all_to_all | solution.py:226
  75.0 0.7 pick.3
  75.7 24.4 %all_to_all.23 = bf16[64,32,512]{2,1,0:T(8,128)(2,1)S(1)} all-to-all(bf16[64,32,512]{2,1,0:T(8,128)(2,1)S(1)} %pick.3), channel_id=1, replica_groups={{0,1,2,3,4,5,6,7,8,9,10,11,12,13,14,15,32,33,34,35,36,37,38,39,40,41,42..., dimensions={0} | all-to-all | bytes 4194304 | tf_op jit(solution)/shard_map/all_to_all | solution.py:38
  100.1 0.1 fusion
  100.3 13.5 %collective-permute-start.5 = (bf16[2,512,512]{2,1,0:T(8,128)(2,1)S(1)}, bf16[2,512,512]{2,1,0:T(8,128)(2,1)S(1)}, u32[]{:S(2)}, u32[]{:S(2)}) collective-permute-start(bf16[2,512,512]{2,1,0:T(8,128)(2,1)S(1)} %bitcast.46), channel_id=1, source_target_pairs={{0,16},{16,0},{32,48},{48,32},{64,80},{80,64},{96,112},{112,96},{1... | collective-permute-start | bytes 3145736 | tf_op jit(solution)/shard_map/swap/ppermute | solution.py:34
  113.7 0.1 collective-permute-start.4
  113.8 0.1 pad_add_fusion.cols_ref
  113.9 0.1 pad_add_fusion.1.cols_ref
  114.0 0.1 pad_add_fusion.2.cols_ref
  114.1 1.9 %store.3.refs_0_ = bf16[512,4096]{1,0:T(8,128)(2,1)} custom-call(s32[4]{0:T(128)S(1)} %pad_add_fusion.2.cols_ref, bf16[4,512,512]{2,1,0:T(8,128)(2,1)S(1)} %bitcast.35), custom_call_target="tpu_custom_call" | custom-call | tf_op jit(solution)/shard_map/store/pallas_call | solution.py:189
  116.0 0.1 collective-permute-done.5.x_ref
  116.0 1.5 %store.4.refs_0_ = bf16[512,4096]{1,0:T(8,128)(2,1)} custom-call(s32[2]{0:T(128)S(1)} %pad_add_fusion.1.cols_ref, bf16[2,512,512]{2,1,0:T(8,128)(2,1)S(1)} %collective-permute-done.5.x_ref, bf16[512,4096]{1,0:T(8,128)(2,1)} %store.3.refs_0_), custom_call_target="tpu_custom_call", output_to_operand_aliasing={{}: (2, {})} | custom-call | tf_op jit(solution)/shard_map/store/pallas_call | solution.py:189
  117.6 0.0 collective-permute-done.4.x_ref
  117.6 1.5 %store.5 = bf16[512,4096]{1,0:T(8,128)(2,1)} custom-call(s32[2]{0:T(128)S(1)} %pad_add_fusion.cols_ref, bf16[2,512,512]{2,1,0:T(8,128)(2,1)S(1)} %collective-permute-done.4.x_ref, bf16[512,4096]{1,0:T(8,128)(2,1)} %store.4.refs_0_), custom_call_target="tpu_custom_call", output_to_operand_aliasing={{}: (2, {})} | custom-call | tf_op jit(solution)/shard_map/store/pallas_call | solution.py:189
  (1 shorter events, 0.0 us)
Async XLA Ops:
  2.0 5.5 %collective-permute-start = (bf16[2,512,512]{2,1,0:T(8,128)(2,1)S(1)}, bf16[2,512,512]{2,1,0:T(8,128)(2,1)S(1)}, u32[]{:S(2)}, u32[]{:S(2)}) collective-permute-start(bf16[2,512,512]{2,1,0:T(8,128)(2,1)S(1)} %pad_maximum_fusion.1), channel_id=1, source_target_pairs={{0,16},{16,0},{32,48},{48,32},{64,80},{80,64},{96,112},{112,96},{1... | collective-permute-start | bytes 3145736 | tf_op jit(solution)/shard_map/swap/ppermute | solution.py:34
  5.7 2.7 %collective-permute-start.1 = (bf16[2,512,512]{2,1,0:T(8,128)(2,1)S(1)}, bf16[2,512,512]{2,1,0:T(8,128)(2,1)S(1)}, u32[]{:S(2)}, u32[]{:S(2)}) collective-permute-start(bf16[2,512,512]{2,1,0:T(8,128)(2,1)S(1)} %pad_maximum_fusion.2), channel_id=1, source_target_pairs={{0,16},{16,0},{32,48},{48,32},{64,80},{80,64},{96,112},{112,96},{1... | collective-permute-start | bytes 3145736 | tf_op jit(solution)/shard_map/swap/ppermute | solution.py:34
  5.8 0.9 collective-permute-start.2
  6.5 1.0 copy-start.3
  6.8 0.8 collective-permute-start.3
  40.8 16.0 %copy-start = (bf16[1,1,2,2,512,512]{5,4,3,2,1,0:T(8,128)(2,1)S(1)}, bf16[1,1,2,2,512,512]{5,4,3,2,1,0:T(8,128)(2,1)}, u32[]{:S(2)}) copy-start(bf16[1,1,2,2,512,512]{5,4,3,2,1,0:T(8,128)(2,1)} %param.7) | copy-start | bytes 6291460
  40.8 16.0 %copy-start.1 = (f32[1,1,2,512,512]{4,3,2,1,0:T(8,128)S(1)}, f32[1,1,2,512,512]{4,3,2,1,0:T(8,128)}, u32[]{:S(2)}) copy-start(f32[1,1,2,512,512]{4,3,2,1,0:T(8,128)} %param.9) | copy-start | bytes 6291460
  40.8 16.0 %copy-start.2 = (bf16[1,1,2,512,512]{4,3,2,1,0:T(8,128)(2,1)S(1)}, bf16[1,1,2,512,512]{4,3,2,1,0:T(8,128)(2,1)}, u32[]{:S(2)}) copy-start(bf16[1,1,2,512,512]{4,3,2,1,0:T(8,128)(2,1)} %param.8) | copy-start | bytes 3145732
  100.3 15.8 %collective-permute-start.5 = (bf16[2,512,512]{2,1,0:T(8,128)(2,1)S(1)}, bf16[2,512,512]{2,1,0:T(8,128)(2,1)S(1)}, u32[]{:S(2)}, u32[]{:S(2)}) collective-permute-start(bf16[2,512,512]{2,1,0:T(8,128)(2,1)S(1)} %bitcast.46), channel_id=1, source_target_pairs={{0,16},{16,0},{32,48},{48,32},{64,80},{80,64},{96,112},{112,96},{1... | collective-permute-start | bytes 3145736 | tf_op jit(solution)/shard_map/swap/ppermute | solution.py:34
  113.7 3.8 %collective-permute-start.4 = (bf16[2,512,512]{2,1,0:T(8,128)(2,1)S(1)}, bf16[2,512,512]{2,1,0:T(8,128)(2,1)S(1)}, u32[]{:S(2)}, u32[]{:S(2)}) collective-permute-start(bf16[2,512,512]{2,1,0:T(8,128)(2,1)S(1)} %bitcast.45), channel_id=1, source_target_pairs={{0,16},{16,0},{32,48},{48,32},{64,80},{80,64},{96,112},{112,96},{1... | collective-permute-start | bytes 3145736 | tf_op jit(solution)/shard_map/swap/ppermute | solution.py:34

commit v5 on v4

--- a/solution.py
+++ b/solution.py
@@ -40,9 +40,10 @@
     )
 
 
-def sum_kernel(own_ref, a_ref, b_ref, after_ref, o_ref):
-    for z, other in enumerate((a_ref[0], a_ref[1], b_ref[0], b_ref[1])):
-        total = own_ref[z].astype(jnp.float32) + other.astype(jnp.float32)
+def sum_kernel(*refs):
+    o_ref = refs[-1]
+    for z in range(4):
+        total = refs[z][...].astype(jnp.float32) + refs[4 + z][...].astype(jnp.float32)
         o_ref[z] = total.astype(jnp.bfloat16)
 
 
@@ -50,16 +51,16 @@
     def part(x, z, which):
         return lax.dynamic_slice(x, (0, (2 * z + which) * SIDE), (SIDE, SIDE))
 
-    give_a = jnp.stack([part(grads, z, 1 - core) for z in (0, 1)])
-    later, give_a = lax.optimization_barrier((grads, give_a))
-    got_a = swap(give_a)
-    got_b = swap(jnp.stack([part(later, z, 1 - core) for z in (2, 3)]))
-    x = give_a[0, :16, :128]
+    give_a = [part(grads, z, 1 - core) for z in (0, 1)]
+    later, *give_a = lax.optimization_barrier((grads, *give_a))
+    got = [swap(x) for x in give_a + [part(later, z, 1 - core) for z in (2, 3)]]
+    x = give_a[0][:16, :128]
     for _ in range(2):
         with jax.named_scope("hop"):
             x = lax.ppermute(x, "replica", NEXT)
-    own = jnp.stack([part(later, z, core) for z in range(4)])
-    return vmem_call(sum_kernel, "sum", jax.ShapeDtypeStruct(own.shape, own.dtype), own, got_a, got_b, x)
+    own = [part(later, z, core) for z in range(4)]
+    shape = jax.ShapeDtypeStruct((4, SIDE, SIDE), grads.dtype)
+    return vmem_call(sum_kernel, "sum", shape, *own, *got, x)
 
 
 def pick_sum_kernel(index_ref, x_ref, o_ref):

time: 119 us -> 119 us (level)
    dynamic_slice x1 -> x2, local copies, waits for them, and re-layouts: 1.28 us -> 3.34 us  [part(): return lax.dynamic_slice(x, (0, (2 * z + which) * SIDE), (SIDE, SIDE))]
    another operation x1 -> x0, local copies, waits for them, and re-layouts: 2.05 us -> none  [core_sums(): got_b = swap(jnp.stack([part(later, z, 1 - core) for z in (2, 3)]))]
    ppermute x4 -> x6, starting transfers between devices: 15.2 us -> 15.8 us  [swap(): return lax.ppermute(x, 'replica', CORES)]
  transfers between devices with their start and end apart: 6 -> 8, of which waited for: 2 -> 2; matrix products, arithmetic and copies ran while one was open for 2% -> 2% of each run, Pallas kernels for 3% -> 3%
where the time goes in v5:
time: 119 us
  blocking collectives  85.5 us (72%)
  starting transfers between devices  17.1 us (14%)
  Pallas kernels  11 us (9%)
  local copies, waits for them, and re-layouts  3.5 us (3%)
    all_to_all x2, blocking collectives, exchange(): lax.all_to_all(x, ('replica', 'fsdp'), 0, 0, tiled=True, axis_index_group...  56 us
    ppermute x6, starting transfers between devices, swap(): return lax.ppermute(x, 'replica', CORES)  15.8 us
    all_to_all x1, blocking collectives, body(): lax.all_to_all(routed.reshape(PEERS, SLOTS, PIECE, SIDE), 'fsdp', 0, 0, t...  15 us
    all_to_all x1, blocking collectives, body(): back = lax.all_to_all(update, 'fsdp', 0, 0, tiled=True)  14.5 us
    pallas_call x3, Pallas kernels, store(): pl.pallas_call(store_kernel, out_shape=jax.ShapeDtypeStruct((SIDE, 8 * SI...  4.95 us
    pallas_call x1, Pallas kernels, slot_step(): pl.pallas_call(slot_kernel, out_shape=(jax.ShapeDtypeStruct(slots, jnp.bf...  3.75 us
    dynamic_slice x2, local copies, waits for them, and re-layouts, part(): return lax.dynamic_slice(x, (0, (2 * z + which) * SIDE), (SIDE, SIDE))  3.34 us
  transfers between devices with their start and end apart: 8, of which 2 were waited for; matrix products, arithmetic and copies ran while one was open for 2% of the time, Pallas kernels for 3%

profile of v5, /device:TPU:1, one launch (start us, length us, event | category | flops | bytes accessed | tf_op | source)
XLA Modules:
  0.0 119.0 jit_solution(6985671913225814888)
XLA Ops:
  0.6 1.3 %dynamic-slice_bitcast_fusion = (bf16[512,512]{1,0:T(8,128)(2,1)S(1)}, bf16[512,512]{1,0:T(8,128)(2,1)S(1)}) fusion(bf16[1,512,4096]{2,1,0:T(8,128)(2,1)} %param.5, s32[]{:T(128)S(6)} %select_n.29, s32[]{:T(128)S(6)} %select_n.28), kind=kLoop, calls=%fused_computation | loop fusion | bytes 2097160 | tf_op jit(solution)/shard_map/dynamic_slice | solution.py:52
  1.9 1.5 %collective-permute-start.1 = (bf16[512,512]{1,0:T(8,128)(2,1)S(1)}, bf16[512,512]{1,0:T(8,128)(2,1)S(1)}, u32[]{:S(2)}, u32[]{:S(2)}) collective-permute-start(bf16[512,512]{1,0:T(8,128)(2,1)S(1)} %get-tuple-element.13), channel_id=1, source_target_pairs={{0,16},{16,0},{32,48},{48,32},{64,80},{80,64},{96,112},{112,96},{1... | collective-permute-start | bytes 1572872 | tf_op jit(solution)/shard_map/swap/ppermute | solution.py:34
  3.4 0.1 collective-permute-start
  3.5 0.0 copy-start.3
  3.5 2.1 %constant_dynamic-slice_fusion = (bf16[512,512]{1,0:T(8,128)(2,1)S(1)}, bf16[512,512]{1,0:T(8,128)(2,1)S(1)}, bf16[512,512]{1,0:T(8,128)(2,1)S(1)}, bf16[512,512...) fusion(bf16[512,4096]{1,0:T(8,128)(2,1)} %bitcast.34, s32[]{:T(128)S(6)} %select_n.35, ...), kind=kLoop, calls=%fused_computation.4 | loop fusion | bytes 6291480 | tf_op jit(solution)/shard_map/dynamic_slice | solution.py:52
  5.6 0.5 collective-permute-start.3
  6.1 0.1 collective-permute-start.2
  6.2 0.6 collective-permute-start.4
  6.8 0.0 collective-permute-done.4
  6.8 0.7 collective-permute-start.5
  7.5 0.0 copy-done.3
  7.5 0.1 select_reduce_fusion.index_ref
  7.6 0.0 collective-permute-done.5.refs_8_
  7.6 0.0 collective-permute-done.1.refs_5_
  7.6 0.0 collective-permute-done.refs_4_
  7.6 0.0 collective-permute-done.3.refs_7_
  7.7 0.7 collective-permute-done.2.refs_6_
  8.4 0.5 sum.1
  8.8 31.3 %all_to_all.20.x_ref = bf16[64,32,512]{2,1,0:T(8,128)(2,1)S(1)} all-to-all(bf16[64,32,512]{2,1,0:T(8,128)(2,1)S(1)} %bitcast.26), channel_id=1, replica_groups={{0,1,2,3,4,5,6,7,8,9,10,11,12,13,14,15,32,33,34,35,36,37,38,39,40,41,42..., dimensions={0} | all-to-all | bytes 4194304 | tf_op jit(solution)/shard_map/all_to_all | solution.py:38
  40.1 0.0 copy-start
  40.1 0.0 copy-start.1
  40.1 0.0 copy-start.2
  40.1 1.2 %pick.2 = bf16[32,32,512]{2,1,0:T(8,128)(2,1)S(1)} custom-call(s32[32]{0:T(128)S(1)} %select_reduce_fusion.index_ref, bf16[64,32,512]{2,1,0:T(8,128)(2,1)S(1)} %all_to_all.20.x_ref), custom_call_target="tpu_custom_call" | custom-call | tf_op jit(solution)/shard_map/pick/pallas_call | solution.py:88
  41.3 15.0 %all_to_all.21.g_ref = bf16[16,2,32,512]{3,2,1,0:T(8,128)(2,1)S(1)} all-to-all(bf16[16,2,32,512]{3,2,1,0:T(8,128)(2,1)S(1)} %bitcast.27), channel_id=1, replica_groups=mesh['replica'=8,'fsdp'=16] {'fsdp'}, dimensions={0} | all-to-all | bytes 2097152 | tf_op jit(solution)/shard_map/all_to_all | solution.py:221
  56.4 0.0 copy-done
  56.4 0.0 copy-done.1
  56.4 0.0 copy-done.2
  56.4 3.7 %slot_step.1 = (bf16[2,512,512]{2,1,0:T(8,128)(2,1)}, f32[2,512,512]{2,1,0:T(8,128)}, bf16[16,2,32,512]{3,2,1,0:T(8,128)(2,1)S(1)}) custom-call(bf16[16,2,32,512]{3,2,1,0:T(8,128)(2,1)S(1)} %all_to_all.21.g_ref, bf16[2,2,512,512]{3,2,1,0:T(8,128)(2,1)S(1)} %bitcast.29, bf16[2,512,512]{2,1,0:T(8,128)(2,1)S(1)} %bitcast.31, f32[2,512,512]{2,1,0:T(8,128)S(1)} %bitcast.30), custom_call_target="tpu_custom_call" | custom-call | tf_op jit(solution)/shard_map/slot_step/pallas_call | solution.py:151
  60.1 14.5 %all_to_all.22 = bf16[16,2,32,512]{3,2,1,0:T(8,128)(2,1)S(1)} all-to-all(bf16[16,2,32,512]{3,2,1,0:T(8,128)(2,1)S(1)} %get-tuple-element.16), channel_id=1, replica_groups=mesh['replica'=8,'fsdp'=16] {'fsdp'}, dimensions={0} | all-to-all | bytes 2097152 | tf_op jit(solution)/shard_map/all_to_all | solution.py:227
  74.6 0.7 pick.3
  75.3 24.7 %all_to_all.23 = bf16[64,32,512]{2,1,0:T(8,128)(2,1)S(1)} all-to-all(bf16[64,32,512]{2,1,0:T(8,128)(2,1)S(1)} %pick.3), channel_id=1, replica_groups={{0,1,2,3,4,5,6,7,8,9,10,11,12,13,14,15,32,33,34,35,36,37,38,39,40,41,42..., dimensions={0} | all-to-all | bytes 4194304 | tf_op jit(solution)/shard_map/all_to_all | solution.py:38
  100.0 0.1 fusion
  100.2 13.5 %collective-permute-start.7 = (bf16[2,512,512]{2,1,0:T(8,128)(2,1)S(1)}, bf16[2,512,512]{2,1,0:T(8,128)(2,1)S(1)}, u32[]{:S(2)}, u32[]{:S(2)}) collective-permute-start(bf16[2,512,512]{2,1,0:T(8,128)(2,1)S(1)} %bitcast.36), channel_id=1, source_target_pairs={{0,16},{16,0},{32,48},{48,32},{64,80},{80,64},{96,112},{112,96},{1... | collective-permute-start | bytes 3145736 | tf_op jit(solution)/shard_map/swap/ppermute | solution.py:34
  113.7 0.1 collective-permute-start.6
  113.8 0.1 pad_add_fusion.cols_ref
  113.9 0.1 pad_add_fusion.1.cols_ref
  113.9 0.1 pad_add_fusion.2.cols_ref
  114.0 1.9 %store.3.refs_0_ = bf16[512,4096]{1,0:T(8,128)(2,1)} custom-call(s32[4]{0:T(128)S(1)} %pad_add_fusion.2.cols_ref, bf16[4,512,512]{2,1,0:T(8,128)(2,1)S(1)} %bitcast.25), custom_call_target="tpu_custom_call" | custom-call | tf_op jit(solution)/shard_map/store/pallas_call | solution.py:190
  115.9 0.1 collective-permute-done.7.x_ref
  116.0 1.5 %store.4.refs_0_ = bf16[512,4096]{1,0:T(8,128)(2,1)} custom-call(s32[2]{0:T(128)S(1)} %pad_add_fusion.1.cols_ref, bf16[2,512,512]{2,1,0:T(8,128)(2,1)S(1)} %collective-permute-done.7.x_ref, bf16[512,4096]{1,0:T(8,128)(2,1)} %store.3.refs_0_), custom_call_target="tpu_custom_call", output_to_operand_aliasing={{}: (2, {})} | custom-call | tf_op jit(solution)/shard_map/store/pallas_call | solution.py:190
  117.5 0.0 collective-permute-done.6.x_ref
  117.5 1.5 %store.5 = bf16[512,4096]{1,0:T(8,128)(2,1)} custom-call(s32[2]{0:T(128)S(1)} %pad_add_fusion.cols_ref, bf16[2,512,512]{2,1,0:T(8,128)(2,1)S(1)} %collective-permute-done.6.x_ref, bf16[512,4096]{1,0:T(8,128)(2,1)} %store.4.refs_0_), custom_call_target="tpu_custom_call", output_to_operand_aliasing={{}: (2, {})} | custom-call | tf_op jit(solution)/shard_map/store/pallas_call | solution.py:190
  (1 shorter events, 0.0 us)
Async XLA Ops:
  1.9 5.7 %collective-permute-start.1 = (bf16[512,512]{1,0:T(8,128)(2,1)S(1)}, bf16[512,512]{1,0:T(8,128)(2,1)S(1)}, u32[]{:S(2)}, u32[]{:S(2)}) collective-permute-start(bf16[512,512]{1,0:T(8,128)(2,1)S(1)} %get-tuple-element.13), channel_id=1, source_target_pairs={{0,16},{16,0},{32,48},{48,32},{64,80},{80,64},{96,112},{112,96},{1... | collective-permute-start | bytes 1572872 | tf_op jit(solution)/shard_map/swap/ppermute | solution.py:34
  3.4 4.2 %collective-permute-start = (bf16[512,512]{1,0:T(8,128)(2,1)S(1)}, bf16[512,512]{1,0:T(8,128)(2,1)S(1)}, u32[]{:S(2)}, u32[]{:S(2)}) collective-permute-start(bf16[512,512]{1,0:T(8,128)(2,1)S(1)} %get-tuple-element.12), channel_id=1, source_target_pairs={{0,16},{16,0},{32,48},{48,32},{64,80},{80,64},{96,112},{112,96},{1... | collective-permute-start | bytes 1572872 | tf_op jit(solution)/shard_map/swap/ppermute | solution.py:34
  3.5 4.0 %copy-start.3 = (s32[16,1]{0,1:T(1,128)S(1)}, s32[16,1]{0,1:T(1,128)}, u32[]{:S(2)}) copy-start(s32[16,1]{0,1:T(1,128)} %param.6) | copy-start | bytes 196
  5.6 2.1 %collective-permute-start.3 = (bf16[512,512]{1,0:T(8,128)(2,1)S(1)}, bf16[512,512]{1,0:T(8,128)(2,1)S(1)}, u32[]{:S(2)}, u32[]{:S(2)}) collective-permute-start(bf16[512,512]{1,0:T(8,128)(2,1)S(1)} %get-tuple-element.19), channel_id=1, source_target_pairs={{0,16},{16,0},{32,48},{48,32},{64,80},{80,64},{96,112},{112,96},{1... | collective-permute-start | bytes 1572872 | tf_op jit(solution)/shard_map/swap/ppermute | solution.py:34
  6.1 2.3 %collective-permute-start.2 = (bf16[512,512]{1,0:T(8,128)(2,1)S(1)}, bf16[512,512]{1,0:T(8,128)(2,1)S(1)}, u32[]{:S(2)}, u32[]{:S(2)}) collective-permute-start(bf16[512,512]{1,0:T(8,128)(2,1)S(1)} %get-tuple-element.20), channel_id=1, source_target_pairs={{0,16},{16,0},{32,48},{48,32},{64,80},{80,64},{96,112},{112,96},{1... | collective-permute-start | bytes 1572872 | tf_op jit(solution)/shard_map/swap/ppermute | solution.py:34
  6.2 0.7 collective-permute-start.4
  6.8 0.8 collective-permute-start.5
  40.1 16.2 %copy-start = (bf16[1,1,2,2,512,512]{5,4,3,2,1,0:T(8,128)(2,1)S(1)}, bf16[1,1,2,2,512,512]{5,4,3,2,1,0:T(8,128)(2,1)}, u32[]{:S(2)}) copy-start(bf16[1,1,2,2,512,512]{5,4,3,2,1,0:T(8,128)(2,1)} %param.7) | copy-start | bytes 6291460
  40.1 16.2 %copy-start.1 = (f32[1,1,2,512,512]{4,3,2,1,0:T(8,128)S(1)}, f32[1,1,2,512,512]{4,3,2,1,0:T(8,128)}, u32[]{:S(2)}) copy-start(f32[1,1,2,512,512]{4,3,2,1,0:T(8,128)} %param.9) | copy-start | bytes 6291460
  40.1 16.2 %copy-start.2 = (bf16[1,1,2,512,512]{4,3,2,1,0:T(8,128)(2,1)S(1)}, bf16[1,1,2,512,512]{4,3,2,1,0:T(8,128)(2,1)}, u32[]{:S(2)}) copy-start(bf16[1,1,2,512,512]{4,3,2,1,0:T(8,128)(2,1)} %param.8) | copy-start | bytes 3145732
  100.2 15.8 %collective-permute-start.7 = (bf16[2,512,512]{2,1,0:T(8,128)(2,1)S(1)}, bf16[2,512,512]{2,1,0:T(8,128)(2,1)S(1)}, u32[]{:S(2)}, u32[]{:S(2)}) collective-permute-start(bf16[2,512,512]{2,1,0:T(8,128)(2,1)S(1)} %bitcast.36), channel_id=1, source_target_pairs={{0,16},{16,0},{32,48},{48,32},{64,80},{80,64},{96,112},{112,96},{1... | collective-permute-start | bytes 3145736 | tf_op jit(solution)/shard_map/swap/ppermute | solution.py:34
  113.7 3.8 %collective-permute-start.6 = (bf16[2,512,512]{2,1,0:T(8,128)(2,1)S(1)}, bf16[2,512,512]{2,1,0:T(8,128)(2,1)S(1)}, u32[]{:S(2)}, u32[]{:S(2)}) collective-permute-start(bf16[2,512,512]{2,1,0:T(8,128)(2,1)S(1)} %bitcast.35), channel_id=1, source_target_pairs={{0,16},{16,0},{32,48},{48,32},{64,80},{80,64},{96,112},{112,96},{1... | collective-permute-start | bytes 3145736 | tf_op jit(solution)/shard_map/swap/ppermute | solution.py:34
